TPU v7x, 32 devices: a whole 2x2x4 slice. The times are simulated.
32 devices in a mesh: pages: 8 (over z, x), queries: 4 (over y, core).
Axes of the slice: x: 2, y: 2, z: 4, core: 2. Of those that a mesh axis runs over, the one named last changes fastest.
Arguments:
- query_tokens: bfloat16 [8, 32, 128], P('pages'), may hold values from -1 to 1
- page_patches: bfloat16 [16, 1536, 128], P('pages', 'queries'), may hold values from -1 to 1, as said below
- patch_counts: int32 [16], P('pages'), may hold values from 512 to 1536, as said below
- positive_page: int32 [8], replicated, may hold values from 0 to 15
Outputs:
- query_loss: float32 [8], replicated
- query_grad: float32 [8, 32, 128], P('pages', 'queries')
- page_grad: float32 [16, 1536, 128], P('pages', 'queries')
Inputs may be any that keep to these rules, and one draw needn't show every extreme that they name: `patch_counts`: each page's number of valid patches; some page has exactly 1536. `page_patches`: slots at or past a page's count hold arbitrary values.
All inputs are finite; a program needn't handle non-finite values.
Results may differ from a plain program's by a relative error of at most 0.0028.
Values may be sent and summed in bfloat16 or wider, within the bound.
No kernel may reach another device: no remote copies, remote signals or barrier semaphores. Data moves between devices by JAX's collectives and lax.ppermute only.
A program may use at most 64 MiB of HBM per device.

v0:
```python
import jax
import jax.numpy as jnp
from jax import lax
from jax.sharding import PartitionSpec as P

smooth_tau = 0.05
page_temp = 0.02
neg_large = -1e30


def combined_all(part, axis, combine):
    gathered = jax.tree.map(lambda a: lax.all_gather(a, axis), part)

    def take(source):
        return jax.tree.map(lambda a: lax.dynamic_index_in_dim(a, source, 0, False), gathered)

    return lax.fori_loop(
        1, lax.axis_size(axis), lambda source, state: combine(state, take(source)), take(0)
    )


def merge_patch(first, second):
    highest = jnp.maximum(first[0], second[0])
    run_total = first[1] * jnp.exp((first[0] - highest) / smooth_tau) + second[1] * jnp.exp(
        (second[0] - highest) / smooth_tau
    )
    return (highest, run_total)


def merge_page(first, second):
    highest = jnp.maximum(first[0], second[0])
    run_total = first[1] * jnp.exp(first[0] - highest) + second[1] * jnp.exp(second[0] - highest)
    return (highest, run_total, first[2] + second[2])


def shards(query_tokens, page_patches, patch_counts, positive_page):
    group_slot = lax.axis_index("queries")
    gathered = lax.all_gather(query_tokens, "pages", axis=0, tiled=True)
    query_count, query_len, embed_width = gathered.shape
    token_rows = gathered.reshape(query_count * query_len, embed_width)
    row_total = token_rows.shape[0]
    block_rows = min(2048, row_total)
    block_count = row_total // block_rows
    page_local, patch_local, _ = page_patches.shape
    tile_rows = min(128, patch_local)
    live_rows = jnp.clip(patch_counts - group_slot * patch_local, 0, patch_local)
    tile_count = (live_rows + tile_rows - 1) // tile_rows
    tile_pos = jnp.arange(tile_rows, dtype=jnp.int32)

    def tile_scores(block_tokens, page_slab, live_count, tile_idx):
        row_start = tile_idx * tile_rows
        patch_tile = lax.dynamic_slice_in_dim(page_slab, row_start, tile_rows, 0)
        valid_mask = row_start + tile_pos < live_count
        similar = jnp.einsum(
            "re,pe->rp", block_tokens, patch_tile, preferred_element_type=jnp.float32
        )
        return (patch_tile, valid_mask, jnp.where(valid_mask[None, :], similar, neg_large))

    highest_list = []
    total_list = []
    score_list = []
    for page_idx in range(page_local):
        page_slab = page_patches[page_idx]
        live_count = live_rows[page_idx]
        steps_here = tile_count[page_idx]

        def forward_block(block_idx, loop_state):
            highest, run_total, score_page = loop_state
            offset = block_idx * block_rows
            block_tokens = lax.dynamic_slice_in_dim(token_rows, offset, block_rows, 0)

            def forward_tile(tile_idx, inner_state):
                run_max, run_sum, score_buf = inner_state
                _, valid_mask, masked = tile_scores(block_tokens, page_slab, live_count, tile_idx)
                new_max = jnp.maximum(run_max, jnp.max(masked, axis=1))
                fresh_terms = jnp.where(
                    valid_mask[None, :], jnp.exp((masked - new_max[:, None]) / smooth_tau), 0.0
                )
                new_sum = run_sum * jnp.exp((run_max - new_max) / smooth_tau) + jnp.sum(
                    fresh_terms, axis=1
                )
                return (new_max, new_sum, score_buf)

            start_state = (
                jnp.full((block_rows,), neg_large, jnp.float32),
                jnp.zeros((block_rows,), jnp.float32),
                score_page,
            )
            run_max, run_sum, score_page = lax.fori_loop(0, steps_here, forward_tile, start_state)
            highest = lax.dynamic_update_slice_in_dim(highest, run_max, offset, 0)
            run_total = lax.dynamic_update_slice_in_dim(run_total, run_sum, offset, 0)
            return (highest, run_total, score_page)

        score_start = jnp.zeros((1, 1), jnp.float32)
        start_page = (
            jnp.full((row_total,), neg_large, jnp.float32),
            jnp.zeros((row_total,), jnp.float32),
            score_start,
        )
        highest, run_total, score_page = lax.fori_loop(0, block_count, forward_block, start_page)
        highest_list.append(highest)
        total_list.append(run_total)
        score_list.append(score_page)
    highest, run_total = combined_all(
        (jnp.stack(highest_list), jnp.stack(total_list)), "queries", merge_patch
    )
    patch_lse = highest + smooth_tau * jnp.log(run_total)
    smooth = patch_lse - smooth_tau * jnp.log(patch_counts.astype(jnp.float32))[:, None]
    logits = smooth.reshape(page_local, query_count, query_len).sum(axis=2) / page_temp
    page_ids = lax.axis_index("pages") * page_local + jnp.arange(page_local, dtype=jnp.int32)
    is_positive = page_ids[:, None] == positive_page[None, :]
    local_max = jnp.max(logits, axis=0)
    local_sum = jnp.sum(jnp.exp(logits - local_max[None, :]), axis=0)
    local_pos = jnp.sum(jnp.where(is_positive, logits, 0.0), axis=0)
    page_max, page_sum, page_pos = combined_all(
        (local_max, local_sum, local_pos), "pages", merge_page
    )
    query_loss = page_max + jnp.log(page_sum) - page_pos
    weights = (
        jnp.exp(logits - page_max[None, :]) / page_sum[None, :] - is_positive.astype(jnp.float32)
    ) / page_temp
    row_weights = jnp.broadcast_to(
        weights[:, :, None], (page_local, query_count, query_len)
    ).reshape(page_local, row_total)
    grad_rows = jnp.zeros((row_total, embed_width), jnp.float32)
    grad_list = []
    for page_idx in range(page_local):
        page_slab = page_patches[page_idx]
        live_count = live_rows[page_idx]
        steps_here = tile_count[page_idx]
        page_lse = patch_lse[page_idx]
        page_weight = row_weights[page_idx]
        score_page = score_list[page_idx]

        def backward_block(block_idx, loop_state):
            grad_all, grad_slab = loop_state
            offset = block_idx * block_rows
            block_tokens = lax.dynamic_slice_in_dim(token_rows, offset, block_rows, 0)
            block_lse = lax.dynamic_slice_in_dim(page_lse, offset, block_rows, 0)
            block_weight = lax.dynamic_slice_in_dim(page_weight, offset, block_rows, 0)

            def backward_tile(tile_idx, inner_state):
                grad_block, slab_grad = inner_state
                row_start = tile_idx * tile_rows
                patch_tile, valid_mask, masked = tile_scores(
                    block_tokens, page_slab, live_count, tile_idx
                )
                prob_tile = jnp.where(
                    valid_mask[None, :], jnp.exp((masked - block_lse[:, None]) / smooth_tau), 0.0
                )
                coef_tile = (block_weight[:, None] * prob_tile).astype(jnp.bfloat16)
                grad_block = grad_block + jnp.dot(
                    coef_tile, patch_tile, preferred_element_type=jnp.float32
                )
                tile_grad = jnp.einsum(
                    "rp,re->pe", coef_tile, block_tokens, preferred_element_type=jnp.float32
                )
                current = lax.dynamic_slice_in_dim(slab_grad, row_start, tile_rows, 0)
                slab_grad = lax.dynamic_update_slice_in_dim(
                    slab_grad, current + tile_grad, row_start, 0
                )
                return (grad_block, slab_grad)

            grad_block = lax.dynamic_slice_in_dim(grad_all, offset, block_rows, 0)
            grad_block, grad_slab = lax.fori_loop(
                0, steps_here, backward_tile, (grad_block, grad_slab)
            )
            grad_all = lax.dynamic_update_slice_in_dim(grad_all, grad_block, offset, 0)
            return (grad_all, grad_slab)

        start_slab = jnp.zeros((patch_local, embed_width), jnp.float32)
        grad_rows, grad_slab = lax.fori_loop(
            0, block_count, backward_block, (grad_rows, start_slab)
        )
        grad_list.append(grad_slab)
    grad_work = jnp.stack(grad_list)
    grad_three = grad_rows.reshape(query_count, query_len, embed_width)
    partial_value = lax.psum_scatter(grad_three, "queries", scatter_dimension=1, tiled=True)
    query_grad = lax.psum_scatter(partial_value, "pages", scatter_dimension=0, tiled=True)
    return (query_loss, query_grad, grad_work)


def solution(mesh):
    in_specs = (P("pages", None, None), P("pages", "queries", None), P("pages"), P())
    out_specs = (P(), P("pages", "queries", None), P("pages", "queries", None))
    return jax.shard_map(shards, mesh=mesh, in_specs=in_specs, out_specs=out_specs, check_vma=False)
```

profile of v0, /device:TPU:0, one launch (start us, length us, event | category | flops | bytes accessed | tf_op | source)
XLA Modules:
  0.0 165.1 jit_solution(3994124822262873397)
XLA Ops:
  7.2 0.6 copy-done.4
  7.9 1.0 slice_bitcast_fusion.1
  8.9 32.3 %all_gather.33 = bf16[8,32,128]{2,1,0:T(8,128)(2,1)S(1)} all-gather(bf16[1,32,128]{2,1,0:T(8,128)(2,1)S(1)} %copy-done.1), channel_id=1, replica_groups=mesh['pages'=8,'queries'=4] {'pages'}, dimensions={0}, use_global_device_ids=true | all-gather | bytes 73728 | tf_op jit(solution)/shard_map/all_gather | solution.py:38
  41.2 0.7 fusion.61
  41.8 5.4 %while.131 = (s32[]{:T(128)}, f32[256]{0:T(256)S(1)}, f32[256]{0:T(256)S(1)}, s32[]{:T(128)}, s32[]{:T(128)}, /*index=5*/bf16[384,128]{1,0:T(8,128)(2,1)S(1)}, b...) while((s32[]{:T(128)}, f32[256]{0:T(256)S(1)}, ...), condition=%wide.region_7.8_spmd.clone, body=%wide.region_4.7_spmd.clone.sunk | while | flops 8586246 | bytes 374703 | solution.py:89
  42.4 0.7 fusion.105
  43.1 0.2 fusion.106
  43.3 0.1 select_reduce_fusion.5
  44.0 0.7 fusion.105
  44.7 0.2 fusion.106
  45.0 0.1 select_reduce_fusion.5
  45.7 0.7 fusion.105
  46.4 0.2 fusion.106
  46.6 0.1 select_reduce_fusion.5
  47.3 5.4 %while.130 = (s32[]{:T(128)}, f32[256]{0:T(256)S(1)}, f32[256]{0:T(256)S(1)}, s32[]{:T(128)}, s32[]{:T(128)}, /*index=5*/bf16[384,128]{1,0:T(8,128)(2,1)S(1)}, b...) while((s32[]{:T(128)}, f32[256]{0:T(256)S(1)}, ...), condition=%wide.region_3.4_spmd.clone, body=%wide.region_0.3_spmd.clone.sunk | while | flops 8586246 | bytes 374703 | solution.py:89
  47.9 0.6 fusion.102
  48.6 0.2 fusion.103
  49.5 0.6 fusion.102
  50.2 0.2 fusion.103
  51.1 0.6 fusion.102
  51.8 0.2 fusion.103
  52.7 5.2 %all-gather.5 = f32[4,2,256]{2,1,0:T(2,128)S(1)} all-gather(f32[1,2,256]{2,1,0:T(2,128)S(1)} %maximum_bitcast_fusion), channel_id=2, replica_groups=mesh['pages'=8,'queries'=4] {'queries'}, dimensions={0}, use_global_device_ids=true | all-gather | bytes 10240 | tf_op jit(solution)/shard_map/all_gather | solution.py:12
  57.9 5.2 %all-gather.6 = f32[4,2,256]{2,1,0:T(2,128)S(1)} all-gather(f32[1,2,256]{2,1,0:T(2,128)S(1)} %maximum_bitcast_fusion.1), channel_id=3, replica_groups=mesh['pages'=8,'queries'=4] {'queries'}, dimensions={0}, use_global_device_ids=true | all-gather | bytes 10240 | tf_op jit(solution)/shard_map/all_gather | solution.py:12
  63.1 0.1 while.128
  63.5 0.4 copy-done.2
  63.9 0.6 fusion.60
  65.2 0.2 dynamic-update-slice
  65.4 0.4 copy-done.3
  65.9 0.2 dynamic-update-slice.1
  66.1 0.2 dynamic-update-slice.2
  66.4 21.3 %all-reduce.4 = (f32[64]{0:T(128)S(1)}, f32[64]{0:T(128)S(1)}, f32[64]{0:T(128)S(1)}) all-reduce(f32[64]{0:T(128)S(1)} %dynamic-update-slice, f32[64]{0:T(128)S(1)} %dynamic-update-slice.1, f32[64]{0:T(128)S(1)} %dynamic-update-slice.2), channel_id=4, replica_groups=mesh['pages'=8,'queries'=4] {'pages'}, use_global_device_ids=true, to_apply=%add | all-reduce | flops 192 | bytes 1536
  87.9 0.3 while.129
  88.3 6.6 %while.132 = (s32[]{:T(128)}, f32[256,128]{1,0:T(8,128)S(1)}, f32[384,128]{1,0:T(8,128)S(1)}, s32[]{:T(128)}, s32[]{:T(128)}, /*index=5*/bf16[384,128]{1,0:T(8,1...) while((s32[]{:T(128)}, f32[256,128]{1,0:T(8,128)S(1)}, ...), condition=%wide.region_17.18_spmd.clone, body=%wide.region_16.17_spmd.clone.sunk | while | flops 25411844 | bytes 792423 | solution.py:165
  89.1 0.6 fusion.113
  89.7 0.2 fusion.114
  89.9 0.2 convolution_add_fusion.6
  90.2 0.1 fusion.115
  91.1 0.6 fusion.113
  91.7 0.2 fusion.114
  91.9 0.2 convolution_add_fusion.6
  92.1 0.1 fusion.115
  93.1 0.6 fusion.113
  93.7 0.2 fusion.114
  93.9 0.2 convolution_add_fusion.6
  94.1 0.1 fusion.115
  94.9 6.6 %while.133 = (s32[]{:T(128)}, f32[256,128]{1,0:T(8,128)S(1)}, f32[384,128]{1,0:T(8,128)S(1)}, s32[]{:T(128)}, s32[]{:T(128)}, /*index=5*/bf16[384,128]{1,0:T(8,1...) while((s32[]{:T(128)}, f32[256,128]{1,0:T(8,128)S(1)}, ...), condition=%wide.region_19.20_spmd.clone, body=%wide.region_18.19_spmd.clone.sunk | while | flops 25411844 | bytes 792423 | solution.py:165
  95.7 0.7 fusion.122
  96.4 0.2 fusion.123
  96.6 0.2 convolution_add_fusion.7
  96.8 0.1 fusion.124
  97.7 0.7 fusion.122
  98.4 0.2 fusion.123
  98.6 0.2 convolution_add_fusion.7
  98.8 0.1 fusion.124
  99.7 0.7 fusion.122
  100.4 0.2 fusion.123
  100.6 0.2 convolution_add_fusion.7
  100.8 0.1 fusion.124
  101.5 0.6 copy-done
  102.2 0.8 pad_maximum_fusion
  103.0 0.5 add_subtract_fusion
  103.5 15.7 %reduce-scatter.2.cloned.1.call-done = f32[8,8,128]{2,1,0:T(8,128)} async-done(((f32[8,32,128]{2,1,0:T(8,128)}), f32[8,8,128]{2,1,0:T(8,128)}) %reduce-scatter.2.cloned.1.call-update) | async-done | bytes 32784 | tf_op jit(solution)/shard_map/reduce_scatter | solution.py:178
  119.2 37.8 %all-reduce.3 = f32[8,8,128]{2,1,0:T(8,128)S(1)} all-reduce(f32[8,8,128]{2,1,0:T(8,128)} %reduce-scatter.2.cloned.1.call-done), channel_id=8, replica_groups=mesh['pages'=8,'queries'=4] {'pages'}, use_global_device_ids=true, to_apply=%region_21.22.clone | all-reduce | flops 8192 | bytes 65536
  157.0 1.2 constant_dynamic-slice_fusion.3
  (79 shorter events, 2.4 us)
Async XLA Ops:
  7.2 112.0 %reduce-scatter.2.cloned.1.call-start = ((), (), s32[]{:S(2)}) async-start(), calls=%async_computation.1 | async-start | bytes 163840 | tf_op jit(solution)/shard_map/reduce_scatter | solution.py:178
  7.2 0.7 copy-start.4
  7.9 1.0 copy-start.1
  63.2 0.7 copy-start.2
  65.2 0.7 copy-start.3
  101.5 0.6 copy-start
Sparse Core Ops, SparseCore 0:
  102.3 16.8 reduce-scatter.1
where the time goes:
time: 165 us
  blocking collectives  102 us (62%)
  waiting for transfers between devices  15.7 us (10%)
  between operations  14.9 us (9%)
  other arithmetic  10.7 us (6%)
  loops' own time  10.1 us (6%)
  local copies, waits for them, and re-layouts  7.51 us (5%)
  matrix products  4.4 us (3%)
    unnamed x2, blocking collectives  59.1 us
    all_gather x1, blocking collectives, shards(): gathered = lax.all_gather(query_tokens, 'pages', axis=0, tiled=True)  32.3 us
    reduce_scatter x1, waiting for transfers between devices, shards(): lax.psum_scatter(grad_three, 'queries', scatter_dimension=1, tiled=True)  15.7 us
    all_gather x2, blocking collectives, combined_all(): gathered = jax.tree.map(lambda a: lax.all_gather(a, axis), part)  10.3 us
    lt x12, other arithmetic, tile_scores(): valid_mask = row_start + tile_pos < live_count  7.99 us
    another operation x2, loops' own time, backward_block(): lax.fori_loop(0, steps_here, backward_tile, (grad_block, grad_slab))  5.03 us
    another operation x2, loops' own time, forward_block(): lax.fori_loop(0, steps_here, forward_tile, start_state)  4.94 us
    unnamed x18, local copies, waits for them, and re-layouts  4.6 us
  transfers between devices with their start and end apart: 1, of which 1 were waited for; matrix products, arithmetic and copies ran while one was open for 1% of the time, Pallas kernels for 0%

commit v1 on v0

v1 whole, which is shorter than its diff:
```python
import functools

import jax
import jax.numpy as jnp
from jax import lax
from jax.experimental import pallas as pl
from jax.experimental.pallas import tpu as pltpu
from jax.sharding import PartitionSpec as P

smooth_tau = 0.05
page_temp = 0.02
neg_large = -1e30
inv_tau = 1.0 / smooth_tau
inv_temp = 1.0 / page_temp
lanes = 128
block_rows = 256
both = ("pages", "queries")


def contract(a, b, dim_a, dim_b):
    return lax.dot_general(
        a, b, (((dim_a,), (dim_b,)), ((), ())), preferred_element_type=jnp.float32
    )


def over_blocks(count, body):
    if count == 1:
        body(0)
    else:
        lax.fori_loop(0, count, lambda b, _: (body(b), 0)[1], 0)


def forward_kernel(sizes, counts, tokens, own, partner, out, scores):
    slots, share, chunk = sizes
    page_local, patch_local, width = own.shape
    query_len = tokens.shape[1]
    block_queries = block_rows // query_len
    block_peers = block_queries * slots // 2
    slot = lax.axis_index("queries")
    parity = lax.rem(slot, 2)
    sources = ((own, slot * patch_local), (partner, (slot + 1 - 2 * parity) * patch_local))
    position = lax.broadcasted_iota(jnp.int32, (chunk, block_rows), 0)
    steps = [
        (source, start, base, index * patch_local + start)
        for index, (source, base) in enumerate(sources)
        for start in range(0, patch_local, chunk)
    ]

    def block(b):
        query_start = pl.multiple_of(b * block_queries, block_queries)
        token_rows = tokens[pl.ds(query_start, block_queries)].reshape(block_rows, width)
        for page in range(page_local):
            count = counts[page]
            running = jnp.full((8, block_rows), neg_large, jnp.float32)
            for source, start, base, place in steps:
                similar = contract(source[page, start : start + chunk], token_rows, 1, 1)
                live = position < count - base - start
                masked = jnp.where(live, similar, neg_large)
                scores[page, place : place + chunk] = masked
                running = jnp.maximum(
                    running, jnp.max(masked.reshape(chunk // 8, 8, block_rows), axis=0)
                )
            highest = jnp.max(running, axis=0, keepdims=True)
            total = jnp.zeros((8, block_rows), jnp.float32)
            mean = jnp.zeros((width, block_rows), jnp.float32)
            for source, start, base, place in steps:
                terms = jnp.exp((scores[page, place : place + chunk] - highest) * inv_tau)
                total = total + jnp.sum(terms.reshape(chunk // 8, 8, block_rows), axis=0)
                coarse = terms.astype(jnp.bfloat16)
                fine = (terms - coarse.astype(jnp.float32)).astype(jnp.bfloat16)
                patch_rows = source[page, start : start + chunk]
                mean = mean + contract(patch_rows, coarse, 0, 0) + contract(patch_rows, fine, 0, 0)
            total = jnp.sum(total, axis=0, keepdims=True)
            any_live = count > (slot - parity) * patch_local
            log_count = jnp.log(jnp.full((1, block_rows), count, jnp.int32).astype(jnp.float32))
            smooth = highest + smooth_tau * (jnp.log(total) - log_count)
            smooth = jnp.where(any_live, smooth, neg_large)
            rows = jnp.transpose(mean / total).reshape(block_peers, 2, share, width)
            mine = jnp.where(parity == 0, rows[:, 0], rows[:, 1])
            peer_start = pl.multiple_of(b * block_peers, block_peers)
            out[pl.ds(peer_start, block_peers), page * share : (page + 1) * share] = mine
            for half in range(block_rows // lanes):
                line = page_local * share + (page * block_rows // lanes) + half
                line = line + b * (page_local * block_rows // lanes)
                part = smooth[:, half * lanes : (half + 1) * lanes]
                out[:, pl.ds(line, 1)] = jnp.broadcast_to(part[None], (out.shape[0], 1, lanes))

    over_blocks(tokens.shape[0] // block_queries, block)


def backward_kernel(sizes, counts, positive, heard, tokens, own, loss, query_grad, page_grad):
    slots, share, chunk = sizes
    page_local, patch_local, width = own.shape
    query_len = tokens.shape[1]
    block_queries = block_rows // query_len
    halves = block_rows // lanes
    half_queries = lanes // query_len
    groups = heard.shape[0] // 2
    stride = heard.shape[1]
    slot = lax.axis_index("queries")
    group = lax.axis_index("pages")
    flat = heard.reshape(heard.shape[0] * stride, lanes)
    same_query = (
        lax.broadcasted_iota(jnp.int32, (lanes, lanes), 0) // query_len
        == lax.broadcasted_iota(jnp.int32, (lanes, lanes), 1) // query_len
    ).astype(jnp.bfloat16)
    group_ids = lax.broadcasted_iota(jnp.int32, (groups, lanes), 0)
    lane_query = lax.broadcasted_iota(jnp.int32, (1, lanes), 1) // query_len
    position = lax.broadcasted_iota(jnp.int32, (chunk, block_rows), 0)
    pages = range(page_local)

    def token_sums(x):
        coarse = x.astype(jnp.bfloat16)
        rest = x - coarse.astype(jnp.float32)
        middle = rest.astype(jnp.bfloat16)
        fine = (rest - middle.astype(jnp.float32)).astype(jnp.bfloat16)
        sums = contract(jnp.concatenate([coarse, middle, fine], axis=0), same_query, 1, 0)
        size = x.shape[0]
        return sums[:size] + sums[size : 2 * size] + sums[2 * size :]

    def mine(x):
        return jnp.sum(jnp.where(group_ids == group, x, 0.0), axis=0, keepdims=True)

    def block(b):
        row_weights = [[] for _ in pages]
        row_lse = [[] for _ in pages]
        shares = []
        for half in range(halves):
            smooth = []
            parts = []
            for page in pages:
                line = page_local * share + page * halves + half + b * (page_local * halves)
                first = flat[pl.ds(line, groups, stride=2 * stride), :]
                second = flat[pl.ds(line + stride, groups, stride=2 * stride), :]
                highest = jnp.maximum(first, second)
                first = jnp.exp((first - highest) * inv_tau)
                second = jnp.exp((second - highest) * inv_tau)
                total = first + second
                smooth.append(highest + smooth_tau * jnp.log(total))
                parts.append((first / total, second / total))
            sums = token_sums(jnp.concatenate(smooth, axis=0)) * inv_temp
            logits = [sums[page * groups : (page + 1) * groups] for page in pages]
            top = functools.reduce(jnp.maximum, logits)
            top = jnp.max(top, axis=0, keepdims=True)
            grown = [jnp.exp(x - top) for x in logits]
            total = jnp.sum(functools.reduce(jnp.add, grown), axis=0, keepdims=True)
            first_query = b * block_queries + half * half_queries
            target = jnp.zeros((1, lanes), jnp.int32)
            for i in range(half_queries):
                target = jnp.where(lane_query == i, positive[first_query + i], target)
            hits = [group_ids * page_local + page == target for page in pages]
            found = functools.reduce(
                jnp.add, [jnp.where(hit, x, 0.0) for hit, x in zip(hits, logits)]
            )
            losses = top + jnp.log(total) - jnp.sum(found, axis=0, keepdims=True)
            for i in range(half_queries):
                loss[first_query + i] = jnp.max(losses[:, i * query_len : (i + 1) * query_len])
            weights = [
                (x / total - jnp.where(hit, 1.0, 0.0)) * inv_temp for hit, x in zip(hits, grown)
            ]
            for page in pages:
                row_weights[page].append(mine(weights[page]))
                row_lse[page].append(mine(smooth[page]))
            shares.append([weights[page] * part for page in pages for part in parts[page]])

        block_tokens = tokens[
            pl.ds(pl.multiple_of(b * block_queries, block_queries), block_queries)
        ].reshape(block_rows, width)
        for page in pages:
            count = counts[page]
            live_count = count - slot * patch_local
            log_count = jnp.log(jnp.full((1, block_rows), count, jnp.int32).astype(jnp.float32))
            page_weight = jnp.concatenate(row_weights[page], axis=1)
            page_lse = jnp.concatenate(row_lse[page], axis=1) + smooth_tau * log_count
            for start in range(0, patch_local, chunk):
                similar = contract(own[page, start : start + chunk], block_tokens, 1, 1)
                coef = page_weight * jnp.exp((similar - page_lse) * inv_tau)
                coef = jnp.where(position < live_count - start, coef, 0.0).astype(jnp.bfloat16)
                grad = contract(coef, block_tokens, 1, 0)
                if tokens.shape[0] > block_queries:
                    grad = grad + jnp.where(b == 0, 0.0, page_grad[page, start : start + chunk])
                page_grad[page, start : start + chunk] = grad

        @pl.when(group // block_queries == b)
        def _():
            row = lax.rem(group, block_queries) * query_len + slot * share
            half = row // lanes
            grad = jnp.zeros((share, width), jnp.float32)
            for index in range(len(shares[0])):
                page, side = index // 2, index % 2
                picked = shares[0][index]
                for other in range(1, halves):
                    picked = jnp.where(half == other, shares[other][index], picked)
                picked = pltpu.roll(picked, lax.rem(lanes - lax.rem(row, lanes), lanes), 1)
                columns = jnp.transpose(picked)[:share]
                for g in range(groups):
                    part = heard[2 * g + side, page * share : (page + 1) * share]
                    grad = grad + columns[:, g : g + 1] * part
            query_grad[0] = grad

    over_blocks(tokens.shape[0] // block_queries, block)


def shards(page_groups, slots, query_tokens, page_patches, patch_counts, positive_page):
    query_local, query_len, width = query_tokens.shape
    page_local, patch_local, _ = page_patches.shape
    query_count = query_local * page_groups
    share = query_len // slots
    chunk = 128
    lines = page_local * share + page_local * query_count * query_len // lanes
    lines = -(-lines // 8) * 8
    peers = page_groups * slots // 2
    sizes = (slots, share, chunk)
    smem = pl.BlockSpec(memory_space=pltpu.SMEM)
    vmem = pl.BlockSpec(memory_space=pltpu.VMEM)
    limit = (16 << 20) + 2 * peers * lines * lanes * 4
    params = pltpu.CompilerParams(vmem_limit_bytes=limit)

    partner = lax.ppermute(page_patches, "queries", [(i, i ^ 1) for i in range(slots)])
    tokens = lax.all_to_all(
        jnp.broadcast_to(query_tokens, (page_groups, query_len, width)), "pages", 0, 0, tiled=True
    )
    told = pl.pallas_call(
        functools.partial(forward_kernel, sizes),
        out_shape=jax.ShapeDtypeStruct((peers, lines, lanes), jnp.float32),
        in_specs=[smem, vmem, vmem, vmem],
        out_specs=vmem,
        scratch_shapes=[pltpu.VMEM((page_local, 2 * patch_local, block_rows), jnp.float32)],
        compiler_params=params,
        name="forward",
    )(patch_counts, tokens, page_patches, partner)
    members = [
        [g * slots + k for g in range(page_groups) for k in range(parity, slots, 2)]
        for parity in range(2)
    ]
    heard = lax.all_to_all(told, both, 0, 0, axis_index_groups=members, tiled=True)
    return pl.pallas_call(
        functools.partial(backward_kernel, sizes),
        out_shape=(
            jax.ShapeDtypeStruct((query_count,), jnp.float32),
            jax.ShapeDtypeStruct((query_local, share, width), jnp.float32),
            jax.ShapeDtypeStruct((page_local, patch_local, width), jnp.float32),
        ),
        in_specs=[smem, smem, vmem, vmem, vmem],
        out_specs=(smem, vmem, vmem),
        compiler_params=params,
        name="backward",
    )(patch_counts, positive_page, heard, tokens, page_patches)


def solution(mesh):
    in_specs = (P("pages", None, None), P("pages", "queries", None), P("pages"), P())
    out_specs = (P(), P("pages", "queries", None), P("pages", "queries", None))
    body = functools.partial(shards, mesh.shape["pages"], mesh.shape["queries"])
    return jax.shard_map(body, mesh=mesh, in_specs=in_specs, out_specs=out_specs, check_vma=False)
```

time: 165 us -> 30.8 us (0.19)
  blocking collectives: 102 us -> 24.6 us
  waiting for transfers between devices: 15.7 us -> 0.01 us
  between operations: 14.9 us -> 0.67 us
  other arithmetic: 10.7 us -> 0 us
  loops' own time: 10.1 us -> 0 us
  local copies, waits for them, and re-layouts: 7.51 us -> 0.72 us
  matrix products: 4.4 us -> 0 us
  Pallas kernels: 0 us -> 4.09 us
    unnamed x2 -> x0, blocking collectives: 59.1 us -> none
    all_gather x3 -> x0, blocking collectives: 42.6 us -> none  [the longest x1 32.3 us: shards(): gathered = lax.all_gather(query_tokens, 'pages', axis=0, tiled=True)]
    all_to_all x0 -> x2, blocking collectives: none -> 24.6 us  [the longest x1 13.5 us: shards(): lax.all_to_all(jnp.broadcast_to(query_tokens, (page_groups, query_len, wi...]
    reduce_scatter x1 -> x0, waiting for transfers between devices: 15.7 us -> none  [shards(): lax.psum_scatter(grad_three, 'queries', scatter_dimension=1, tiled=True)]
    another operation x6 -> x0, loops' own time: 10.1 us -> none  [the longest x2 5.03 us: backward_block(): lax.fori_loop(0, steps_here, backward_tile, (grad_block, grad_slab))]
    lt x12 -> x0, other arithmetic: 7.99 us -> none  [tile_scores(): valid_mask = row_start + tile_pos < live_count]
    unnamed x18 -> x6, local copies, waits for them, and re-layouts: 4.6 us -> 0.02 us
    dot_general x24 -> x0, matrix products: 4.4 us -> none  [the longest x12 2.3 us: tile_scores(): jnp.einsum('re,pe->rp', block_tokens, patch_tile, preferred_element_type=...]
  transfers between devices with their start and end apart: 1 -> 1, of which waited for: 1 -> 0; matrix products, arithmetic and copies ran while one was open for 1% -> 2% of each run, Pallas kernels for 0% -> 0%
where the time goes in v1:
time: 30.8 us; the launch traced here: 30.6 us
  blocking collectives  24.6 us (80%)
  Pallas kernels  4.09 us (13%)
  local copies, waits for them, and re-layouts  0.72 us (2%)
  between operations  0.67 us (2%)
  starting transfers between devices  0.52 us (2%)
    all_to_all x1, blocking collectives, shards(): lax.all_to_all(jnp.broadcast_to(query_tokens, (page_groups, query_len, wi...  13.5 us
    all_to_all x1, blocking collectives, shards(): lax.all_to_all(told, both, 0, 0, axis_index_groups=members, tiled=True)  11 us
    pallas_call x1, Pallas kernels, shards(): pl.pallas_call(functools.partial(backward_kernel, sizes), out_shape=(jax....  2.23 us
    pallas_call x1, Pallas kernels, shards(): pl.pallas_call(functools.partial(forward_kernel, sizes), out_shape=jax.Sh...  1.86 us
    broadcast_in_dim x1, local copies, waits for them, and re-layouts, shards(): jnp.broadcast_to(query_tokens, (page_groups, query_len, width))  0.71 us
  transfers between devices with their start and end apart: 1, of which 0 were waited for; matrix products, arithmetic and copies ran while one was open for 2% of the time, Pallas kernels for 0%

profile of v1, /device:TPU:0, one launch (start us, length us, event | category | flops | bytes accessed | tf_op | source)
XLA Modules:
  0.0 30.6 jit_solution(5479526106015124266)
XLA Ops:
  0.6 0.0 copy-start
  0.6 0.5 %collective-permute-start = (bf16[2,384,128]{2,1,0:T(8,128)(2,1)}, bf16[2,384,128]{2,1,0:T(8,128)(2,1)S(1)}, u32[]{:S(2)}, u32[]{:S(2)}) collective-permute-start(bf16[2,384,128]{2,1,0:T(8,128)(2,1)} %own.3), channel_id=1, source_target_pairs={{0,1},{1,0},{2,3},{3,2},{4,5},{5,4},{6,7},{7,6},{8,9},{9,8},{10,11... | collective-permute-start | bytes 589832 | tf_op jit(solution)/shard_map/ppermute | solution.py:219
  1.2 0.7 %broadcast_in_dim.8 = bf16[8,32,128]{2,1,0:T(8,128)(2,1)S(1)} broadcast(bf16[32,128]{1,0:T(8,128)(2,1)} %bitcast.1), dimensions={1,2} | broadcast | bytes 73728 | tf_op jit(solution)/shard_map/broadcast_in_dim | solution.py:221
  1.9 0.0 copy-start.1
  1.9 13.5 %all_to_all.10.tokens = bf16[8,32,128]{2,1,0:T(8,128)(2,1)S(1)} all-to-all(bf16[8,32,128]{2,1,0:T(8,128)(2,1)S(1)} %broadcast_in_dim.8), channel_id=1, replica_groups=mesh['pages'=8,'queries'=4] {'pages'}, dimensions={0} | all-to-all | bytes 131072 | tf_op jit(solution)/shard_map/all_to_all | solution.py:220
  15.4 0.0 collective-permute-done.partner
  15.4 0.0 copy-done
  15.4 0.0 copy-done.1
  15.4 1.9 %forward.1 = f32[16,24,128]{2,1,0:T(8,128)S(1)} custom-call(s32[2]{0:T(128)S(1)} %copy-done.1, bf16[8,32,128]{2,1,0:T(8,128)(2,1)S(1)} %all_to_all.10.tokens, bf16[2,384,128]{2,1,0:T(8,128)(2,1)S(1)} %copy-done, bf16[2,384,128]{2,1,0:T(8,128)(2,1)S(1)} %collective-permute-done.partner), custom_call_target="tpu_custom_call" | custom-call | tf_op jit(solution)/shard_map/forward/pallas_call | solution.py:223
  17.3 0.0 copy-start.2
  17.3 11.0 %all_to_all.11.heard = f32[16,24,128]{2,1,0:T(8,128)S(1)} all-to-all(f32[16,24,128]{2,1,0:T(8,128)S(1)} %forward.1), channel_id=1, replica_groups={{0,2,4,6,8,10,12,14,16,18,20,22,24,26,28,30},{1,3,5,7,9,11,13,15,17,19,..., dimensions={0} | all-to-all | bytes 393216 | tf_op jit(solution)/shard_map/all_to_all | solution.py:236
  28.3 0.0 copy-done.2
  28.3 2.2 %backward.1 = (f32[8]{0:T(128)}, f32[1,8,128]{2,1,0:T(8,128)}, f32[2,384,128]{2,1,0:T(8,128)}) custom-call(s32[2]{0:T(128)S(1)} %copy-done.1, s32[8]{0:T(128)S(1)} %copy-done.2, f32[16,24,128]{2,1,0:T(8,128)S(1)} %all_to_all.11.heard, bf16[8,32,128]{2,1,0:T(8,128)(2,1)S(1)} %all_to_all.10.tokens, bf16[2,384,128]{2,1,0:T(8,128)(2,1)S(1)} %copy-done), custom_call_target="tpu_custom_call" | custom-call | tf_op jit(solution)/shard_map/backward/pallas_call | solution.py:237
Async XLA Ops:
  0.6 14.8 %copy-start = (bf16[2,384,128]{2,1,0:T(8,128)(2,1)S(1)}, bf16[2,384,128]{2,1,0:T(8,128)(2,1)}, u32[]{:S(2)}) copy-start(bf16[2,384,128]{2,1,0:T(8,128)(2,1)} %own.3) | copy-start | bytes 589828
  0.6 14.8 %collective-permute-start = (bf16[2,384,128]{2,1,0:T(8,128)(2,1)}, bf16[2,384,128]{2,1,0:T(8,128)(2,1)S(1)}, u32[]{:S(2)}, u32[]{:S(2)}) collective-permute-start(bf16[2,384,128]{2,1,0:T(8,128)(2,1)} %own.3), channel_id=1, source_target_pairs={{0,1},{1,0},{2,3},{3,2},{4,5},{5,4},{6,7},{7,6},{8,9},{9,8},{10,11... | collective-permute-start | bytes 589832 | tf_op jit(solution)/shard_map/ppermute | solution.py:219
  1.9 13.6 %copy-start.1 = (s32[2]{0:T(128)S(1)}, s32[2]{0:T(128)}, u32[]{:S(2)}) copy-start(s32[2]{0:T(128)} %counts.3) | copy-start | bytes 28
  17.3 11.0 %copy-start.2 = (s32[8]{0:T(128)S(1)}, s32[8]{0:T(128)}, u32[]{:S(2)}) copy-start(s32[8]{0:T(128)} %positive.1) | copy-start | bytes 100

commit v2 on v1

v2 whole, which is shorter than its diff:
```python
import functools
import math

import jax
import jax.numpy as jnp
from jax import lax
from jax.experimental import pallas as pl
from jax.experimental.pallas import tpu as pltpu
from jax.sharding import PartitionSpec as P

smooth_tau = 0.05
page_temp = 0.02
neg_large = -1e30
inv_tau = 1.0 / smooth_tau
inv_temp = 1.0 / page_temp
lanes = 128
block_rows = 256
chunk = 128
both = ("pages", "queries")


def contract(a, b, dim_a, dim_b):
    return lax.dot_general(
        a, b, (((dim_a,), (dim_b,)), ((), ())), preferred_element_type=jnp.float32
    )


def over_blocks(count, body):
    if count == 1:
        body(0)
    else:
        lax.fori_loop(0, count, lambda b, _: (body(b), 0)[1], 0)


def block_of_tokens(tokens, b):
    count = block_rows // tokens.shape[1]
    start = pl.multiple_of(b * count, count)
    return tokens[pl.ds(start, count)].reshape(block_rows, tokens.shape[2])


def integer_rows(counts, positive, rows):
    counts, positive = counts[...][None], positive[...][None]
    lists = [jnp.broadcast_to(counts[:, i : i + 1], (1, rows)) for i in range(counts.shape[1])]
    query_count = positive.shape[1]
    row_query = lax.broadcasted_iota(jnp.int32, (1, rows), 1) // (rows // query_count)
    target = jnp.zeros((1, rows), jnp.int32)
    for query in range(query_count):
        target = jnp.where(row_query == query, positive[:, query : query + 1], target)
    return jnp.concatenate([*lists, target], axis=0)


def log_row(count):
    return jnp.log(count.astype(jnp.float32))


def forward_kernel(share, lines, counts, positive, tokens, own, partner, out, integers, scores):
    page_local, patch_local, width = own.shape
    halves = block_rows // lanes
    block_peers = block_rows // share
    peers = out.shape[0] // lines
    pair_pages = page_local // 2
    slot = lax.axis_index("queries")
    parity = lax.rem(slot, 2)
    sources = ((own, slot * patch_local), (partner, (slot + 1 - 2 * parity) * patch_local))
    position = lax.broadcasted_iota(jnp.int32, (chunk, block_rows), 0)
    steps = [
        (source, start, base, index * patch_local + start)
        for index, (source, base) in enumerate(sources)
        for start in range(0, patch_local, chunk)
    ]

    integers[...] = integer_rows(counts, positive, integers.shape[1])

    def block(b):
        token_rows = block_of_tokens(tokens, b)
        for index in range(pair_pages):
            page = parity * pair_pages + index
            count = integers[pl.ds(page, 1), :block_rows]
            running = jnp.full((8, block_rows), neg_large, jnp.float32)
            for source, start, base, place in steps:
                similar = contract(source[page, start : start + chunk], token_rows, 1, 1)
                live = position < count - base - start
                masked = jnp.where(live, similar, neg_large)
                scores[place : place + chunk] = masked
                running = jnp.maximum(
                    running, jnp.max(masked.reshape(chunk // 8, 8, block_rows), axis=0)
                )
            highest = jnp.max(running, axis=0, keepdims=True)
            total = jnp.zeros((8, block_rows), jnp.float32)
            mean = jnp.zeros((width, block_rows), jnp.float32)
            for source, start, base, place in steps:
                terms = jnp.exp((scores[place : place + chunk] - highest) * inv_tau)
                total = total + jnp.sum(terms.reshape(chunk // 8, 8, block_rows), axis=0)
                coarse = terms.astype(jnp.bfloat16)
                fine = (terms - coarse.astype(jnp.float32)).astype(jnp.bfloat16)
                patch_rows = source[page, start : start + chunk]
                mean = mean + contract(patch_rows, coarse, 0, 0) + contract(patch_rows, fine, 0, 0)
            total = jnp.sum(total, axis=0, keepdims=True)
            any_live = count > (slot - parity) * patch_local
            smooth = highest + smooth_tau * (jnp.log(total) - log_row(count))
            smooth = jnp.where(any_live, smooth, neg_large)
            rows = jnp.transpose(mean / total)
            for i in range(block_peers):
                line = (b * block_peers + i) * lines + index * share
                out[pl.ds(line, share)] = rows[i * share : (i + 1) * share]
            for half in range(halves):
                line = pair_pages * share + (b * pair_pages + index) * halves + half
                part = smooth[:, half * lanes : (half + 1) * lanes]
                out[pl.ds(line, peers, stride=lines)] = jnp.broadcast_to(part, (peers, lanes))

    over_blocks(tokens.shape[0] * tokens.shape[1] // block_rows, block)


def backward_kernel(
    slots, share, lines, integers, heard, tokens, own, loss, query_grad, page_grad
):
    page_local, patch_local, width = own.shape
    query_len = tokens.shape[1]
    block_queries = block_rows // query_len
    halves = block_rows // lanes
    half_queries = lanes // query_len
    pair_pages = page_local // 2
    groups = heard.shape[0] // (lines * slots)
    sides = slots // 2
    slot = lax.axis_index("queries")
    group = lax.axis_index("pages")
    same_query = (
        lax.broadcasted_iota(jnp.int32, (lanes, lanes), 0) // query_len
        == lax.broadcasted_iota(jnp.int32, (lanes, lanes), 1) // query_len
    ).astype(jnp.bfloat16)
    group_ids = lax.broadcasted_iota(jnp.int32, (groups, lanes), 0)
    position = lax.broadcasted_iota(jnp.int32, (chunk, block_rows), 0)
    pages = range(page_local)

    def sender(page, side):
        return 2 * side + page // pair_pages

    def token_sums(x):
        coarse = x.astype(jnp.bfloat16)
        rest = x - coarse.astype(jnp.float32)
        middle = rest.astype(jnp.bfloat16)
        fine = (rest - middle.astype(jnp.float32)).astype(jnp.bfloat16)
        sums = contract(jnp.concatenate([coarse, middle, fine], axis=0), same_query, 1, 0)
        size = x.shape[0]
        return sums[:size] + sums[size : 2 * size] + sums[2 * size :]

    def mine(x):
        return jnp.sum(jnp.where(group_ids == group, x, 0.0), axis=0, keepdims=True)

    def block(b):
        row_weights = [[] for _ in pages]
        row_lse = [[] for _ in pages]
        shares = []
        for half in range(halves):
            smooth = []
            parts = []
            for page in pages:
                line = pair_pages * share + (b * pair_pages + page % pair_pages) * halves + half
                heights = [
                    heard[pl.ds(sender(page, side) * lines + line, groups, stride=slots * lines)]
                    for side in range(sides)
                ]
                highest = functools.reduce(jnp.maximum, heights)
                terms = [jnp.exp((x - highest) * inv_tau) for x in heights]
                total = functools.reduce(jnp.add, terms)
                smooth.append(highest + smooth_tau * jnp.log(total))
                parts.append([x / total for x in terms])
            sums = token_sums(jnp.concatenate(smooth, axis=0)) * inv_temp
            logits = [sums[page * groups : (page + 1) * groups] for page in pages]
            top = functools.reduce(jnp.maximum, logits)
            top = jnp.max(top, axis=0, keepdims=True)
            grown = [jnp.exp(x - top) for x in logits]
            total = jnp.sum(functools.reduce(jnp.add, grown), axis=0, keepdims=True)
            first_query = b * block_queries + half * half_queries
            line = pl.multiple_of(first_query * query_len, lanes)
            target = integers[page_local : page_local + 1, pl.ds(line, lanes)]
            hits = [group_ids * page_local + page == target for page in pages]
            found = functools.reduce(
                jnp.add, [jnp.where(hit, x, 0.0) for hit, x in zip(hits, logits)]
            )
            losses = top + jnp.log(total) - jnp.sum(found, axis=0, keepdims=True)
            for i in range(half_queries):
                loss[first_query + i] = jnp.max(losses[:, i * query_len : (i + 1) * query_len])
            weights = [
                (x / total - jnp.where(hit, 1.0, 0.0)) * inv_temp for hit, x in zip(hits, grown)
            ]
            for page in pages:
                row_weights[page].append(mine(weights[page]))
                row_lse[page].append(mine(smooth[page]))
            shares.append([[weights[page] * part for part in parts[page]] for page in pages])

        token_rows = block_of_tokens(tokens, b)
        for page in pages:
            count = integers[page : page + 1, :block_rows]
            live_count = count - slot * patch_local
            page_weight = jnp.concatenate(row_weights[page], axis=1)
            page_lse = jnp.concatenate(row_lse[page], axis=1) + smooth_tau * log_row(count)
            for start in range(0, patch_local, chunk):
                similar = contract(own[page, start : start + chunk], token_rows, 1, 1)
                coef = page_weight * jnp.exp((similar - page_lse) * inv_tau)
                coef = jnp.where(position < live_count - start, coef, 0.0).astype(jnp.bfloat16)
                grad = contract(coef, token_rows, 1, 0)
                if tokens.shape[0] > block_queries:
                    grad = grad + jnp.where(b == 0, 0.0, page_grad[page, start : start + chunk])
                page_grad[page, start : start + chunk] = grad

        @pl.when(group // block_queries == b)
        def _():
            row = lax.rem(group, block_queries) * query_len + slot * share
            half = row // lanes
            grad = jnp.zeros((share, width), jnp.float32)
            for page in pages:
                for side in range(sides):
                    picked = shares[0][page][side]
                    for other in range(1, halves):
                        picked = jnp.where(half == other, shares[other][page][side], picked)
                    picked = pltpu.roll(picked, lax.rem(lanes - lax.rem(row, lanes), lanes), 1)
                    columns = jnp.transpose(picked)[:share]
                    for g in range(groups):
                        line = (g * slots + sender(page, side)) * lines
                        line = line + page % pair_pages * share
                        grad = grad + columns[:, g : g + 1] * heard[line : line + share]
            query_grad[0] = grad

    over_blocks(tokens.shape[0] // block_queries, block)


def shards(page_groups, slots, query_tokens, page_patches, patch_counts, positive_page):
    query_local, query_len, width = query_tokens.shape
    page_local, patch_local, _ = page_patches.shape
    query_count = query_local * page_groups
    share = query_len // slots
    peers = page_groups * slots
    lines = page_local // 2 * (share + query_count * query_len // lanes)
    tile = math.gcd(lines, 8)
    smem = pl.BlockSpec(memory_space=pltpu.SMEM)
    vmem = pl.BlockSpec(memory_space=pltpu.VMEM)
    limit = (16 << 20) + 2 * peers * lines * lanes * 4
    params = pltpu.CompilerParams(vmem_limit_bytes=limit)

    partner = lax.ppermute(page_patches, "queries", [(i, i ^ 1) for i in range(slots)])
    tokens = lax.all_to_all(
        jnp.broadcast_to(query_tokens, (page_groups, query_len, width)), "pages", 0, 0, tiled=True
    )
    told, integers = pl.pallas_call(
        functools.partial(forward_kernel, share, lines),
        out_shape=(
            jax.ShapeDtypeStruct((peers * lines, lanes), jnp.float32),
            jax.ShapeDtypeStruct((page_local + 1, query_count * query_len), jnp.int32),
        ),
        in_specs=[vmem] * 5,
        out_specs=(vmem, vmem),
        scratch_shapes=[pltpu.VMEM((2 * patch_local, block_rows), jnp.float32)],
        compiler_params=params,
        name="forward",
    )(patch_counts, positive_page, tokens, page_patches, partner)
    told = told.reshape(peers, lines // tile, tile, lanes)
    heard = lax.all_to_all(told, both, 0, 0, tiled=True).reshape(peers * lines, lanes)
    return pl.pallas_call(
        functools.partial(backward_kernel, slots, share, lines),
        out_shape=(
            jax.ShapeDtypeStruct((query_count,), jnp.float32),
            jax.ShapeDtypeStruct((query_local, share, width), jnp.float32),
            jax.ShapeDtypeStruct((page_local, patch_local, width), jnp.float32),
        ),
        in_specs=[vmem] * 4,
        out_specs=(smem, vmem, vmem),
        compiler_params=params,
        name="backward",
    )(integers, heard, tokens, page_patches)


def solution(mesh):
    in_specs = (P("pages", None, None), P("pages", "queries", None), P("pages"), P())
    out_specs = (P(), P("pages", "queries", None), P("pages", "queries", None))
    body = functools.partial(shards, mesh.shape["pages"], mesh.shape["queries"])
    return jax.shard_map(body, mesh=mesh, in_specs=in_specs, out_specs=out_specs, check_vma=False)
```

time: 30.8 us -> 29 us (0.942)
  Pallas kernels: 4.09 us -> 2.73 us
  blocking collectives: 24.6 us -> 24.1 us
    pallas_call x2, Pallas kernels: 4.09 us -> 2.73 us  [the longest x1 1.69 us: shards(): pl.pallas_call(functools.partial(backward_kernel, slots, share, lines), o...]
    all_to_all x1, blocking collectives: 11 us -> 10.5 us  [shards(): lax.all_to_all(told, both, 0, 0, tiled=True).reshape(peers * lines, lanes)]
where the time goes in v2:
time: 29 us; the launch traced here: 28.7 us
  blocking collectives  24.1 us (83%)
  Pallas kernels  2.73 us (9%)
  local copies, waits for them, and re-layouts  0.72 us (2%)
  between operations  0.68 us (2%)
  starting transfers between devices  0.52 us (2%)
    all_to_all x1, blocking collectives, shards(): lax.all_to_all(jnp.broadcast_to(query_tokens, (page_groups, query_len, wi...  13.5 us
    all_to_all x1, blocking collectives, shards(): lax.all_to_all(told, both, 0, 0, tiled=True).reshape(peers * lines, lanes)  10.5 us
    pallas_call x1, Pallas kernels, shards(): pl.pallas_call(functools.partial(backward_kernel, slots, share, lines), o...  1.69 us
    pallas_call x1, Pallas kernels, shards(): pl.pallas_call(functools.partial(forward_kernel, share, lines), out_shape...  1.05 us
    broadcast_in_dim x1, local copies, waits for them, and re-layouts, shards(): jnp.broadcast_to(query_tokens, (page_groups, query_len, width))  0.71 us
  transfers between devices with their start and end apart: 1, of which 0 were waited for; matrix products, arithmetic and copies ran while one was open for 2% of the time, Pallas kernels for 0%

profile of v2, /device:TPU:0, one launch (start us, length us, event | category | flops | bytes accessed | tf_op | source)
XLA Modules:
  0.0 28.7 jit_solution(9861111371065597223)
XLA Ops:
  0.6 0.0 copy-start
  0.6 0.5 %collective-permute-start = (bf16[2,384,128]{2,1,0:T(8,128)(2,1)}, bf16[2,384,128]{2,1,0:T(8,128)(2,1)S(1)}, u32[]{:S(2)}, u32[]{:S(2)}) collective-permute-start(bf16[2,384,128]{2,1,0:T(8,128)(2,1)} %own.3), channel_id=1, source_target_pairs={{0,1},{1,0},{2,3},{3,2},{4,5},{5,4},{6,7},{7,6},{8,9},{9,8},{10,11... | collective-permute-start | bytes 589832 | tf_op jit(solution)/shard_map/ppermute | solution.py:241
  1.2 0.7 %broadcast_in_dim.8 = bf16[8,32,128]{2,1,0:T(8,128)(2,1)S(1)} broadcast(bf16[32,128]{1,0:T(8,128)(2,1)} %bitcast.5), dimensions={1,2} | broadcast | bytes 73728 | tf_op jit(solution)/shard_map/broadcast_in_dim | solution.py:243
  1.9 0.0 copy-start.1
  1.9 0.0 copy-start.2
  1.9 13.5 %all_to_all.10.tokens = bf16[8,32,128]{2,1,0:T(8,128)(2,1)S(1)} all-to-all(bf16[8,32,128]{2,1,0:T(8,128)(2,1)S(1)} %broadcast_in_dim.8), channel_id=1, replica_groups=mesh['pages'=8,'queries'=4] {'pages'}, dimensions={0} | all-to-all | bytes 131072 | tf_op jit(solution)/shard_map/all_to_all | solution.py:242
  15.4 0.0 collective-permute-done.partner
  15.4 0.0 copy-done
  15.4 0.0 copy-done.1
  15.4 0.0 copy-done.2
  15.5 1.0 %forward.1 = (f32[320,128]{1,0:T(8,128)S(1)}, s32[3,256]{1,0:T(4,128)S(1)}) custom-call(s32[2]{0:T(128)S(1)} %copy-done.1, s32[8]{0:T(128)S(1)} %copy-done.2, bf16[8,32,128]{2,1,0:T(8,128)(2,1)S(1)} %all_to_all.10.tokens, bf16[2,384,128]{2,1,0:T(8,128)(2,1)S(1)} %copy-done, bf16[2,384,128]{2,1,0:T(8,128)(2,1)S(1)} %collective-permute-done.partner), custom_call_target="tpu_custom_call" | custom-call | tf_op jit(solution)/shard_map/forward/pallas_call | solution.py:245
  16.5 10.5 %all_to_all.11 = f32[32,5,2,128]{3,2,1,0:T(2,128)S(1)} all-to-all(f32[32,5,2,128]{3,2,1,0:T(2,128)S(1)} %bitcast.4), channel_id=1, replica_groups=mesh['pages'=8,'queries'=4] {'pages','queries'}, dimensions={0} | all-to-all | bytes 327680 | tf_op jit(solution)/shard_map/all_to_all | solution.py:258
  27.0 1.7 %backward.1 = (f32[8]{0:T(128)}, f32[1,8,128]{2,1,0:T(8,128)}, f32[2,384,128]{2,1,0:T(8,128)}) custom-call(s32[3,256]{1,0:T(4,128)S(1)} %get-tuple-element.5.integers, f32[320,128]{1,0:T(8,128)S(1)} %bitcast.3, bf16[8,32,128]{2,1,0:T(8,128)(2,1)S(1)} %all_to_all.10.tokens, bf16[2,384,128]{2,1,0:T(8,128)(2,1)S(1)} %copy-done), custom_call_target="tpu_custom_call" | custom-call | tf_op jit(solution)/shard_map/backward/pallas_call | solution.py:259
Async XLA Ops:
  0.6 14.8 %copy-start = (bf16[2,384,128]{2,1,0:T(8,128)(2,1)S(1)}, bf16[2,384,128]{2,1,0:T(8,128)(2,1)}, u32[]{:S(2)}) copy-start(bf16[2,384,128]{2,1,0:T(8,128)(2,1)} %own.3) | copy-start | bytes 589828
  0.6 14.8 %collective-permute-start = (bf16[2,384,128]{2,1,0:T(8,128)(2,1)}, bf16[2,384,128]{2,1,0:T(8,128)(2,1)S(1)}, u32[]{:S(2)}, u32[]{:S(2)}) collective-permute-start(bf16[2,384,128]{2,1,0:T(8,128)(2,1)} %own.3), channel_id=1, source_target_pairs={{0,1},{1,0},{2,3},{3,2},{4,5},{5,4},{6,7},{7,6},{8,9},{9,8},{10,11... | collective-permute-start | bytes 589832 | tf_op jit(solution)/shard_map/ppermute | solution.py:241
  1.9 13.6 %copy-start.1 = (s32[2]{0:T(128)S(1)}, s32[2]{0:T(128)}, u32[]{:S(2)}) copy-start(s32[2]{0:T(128)} %counts.1) | copy-start | bytes 28
  1.9 13.6 %copy-start.2 = (s32[8]{0:T(128)S(1)}, s32[8]{0:T(128)}, u32[]{:S(2)}) copy-start(s32[8]{0:T(128)} %positive.1) | copy-start | bytes 100

commit v3 on v2

--- a/solution.py
+++ b/solution.py
@@ -13,6 +13,7 @@
 neg_large = -1e30
 inv_tau = 1.0 / smooth_tau
 inv_temp = 1.0 / page_temp
+inv_tau_log2 = inv_tau / math.log(2.0)
 lanes = 128
 block_rows = 256
 chunk = 128
@@ -53,60 +54,66 @@
     return jnp.log(count.astype(jnp.float32))
 
 
-def forward_kernel(share, lines, counts, positive, tokens, own, partner, out, integers, scores):
+def forward_kernel(
+    share, lines, counts, positive, tokens, own, partner, out, integers, scores
+):
     page_local, patch_local, width = own.shape
-    halves = block_rows // lanes
     block_peers = block_rows // share
     peers = out.shape[0] // lines
     pair_pages = page_local // 2
     slot = lax.axis_index("queries")
     parity = lax.rem(slot, 2)
     sources = ((own, slot * patch_local), (partner, (slot + 1 - 2 * parity) * patch_local))
-    position = lax.broadcasted_iota(jnp.int32, (chunk, block_rows), 0)
-    steps = [
-        (source, start, base, index * patch_local + start)
-        for index, (source, base) in enumerate(sources)
-        for start in range(0, patch_local, chunk)
-    ]
-
+    position = lax.broadcasted_iota(jnp.int32, (1, lanes), 1)
+    diagonal = lax.broadcasted_iota(jnp.int32, (lanes, lanes), 0) == lax.broadcasted_iota(
+        jnp.int32, (lanes, lanes), 1
+    )
+    places = [slice(start, start + lanes) for start in range(0, patch_local, lanes)]
     integers[...] = integer_rows(counts, positive, integers.shape[1])
+
+    def as_row(column):
+        return jnp.sum(jnp.where(diagonal, column, 0.0), axis=0, keepdims=True)
 
     def block(b):
         token_rows = block_of_tokens(tokens, b)
         for index in range(pair_pages):
             page = parity * pair_pages + index
-            count = integers[pl.ds(page, 1), :block_rows]
-            running = jnp.full((8, block_rows), neg_large, jnp.float32)
-            for source, start, base, place in steps:
-                similar = contract(source[page, start : start + chunk], token_rows, 1, 1)
-                live = position < count - base - start
-                masked = jnp.where(live, similar, neg_large)
-                scores[place : place + chunk] = masked
-                running = jnp.maximum(
-                    running, jnp.max(masked.reshape(chunk // 8, 8, block_rows), axis=0)
-                )
-            highest = jnp.max(running, axis=0, keepdims=True)
-            total = jnp.zeros((8, block_rows), jnp.float32)
-            mean = jnp.zeros((width, block_rows), jnp.float32)
-            for source, start, base, place in steps:
-                terms = jnp.exp((scores[place : place + chunk] - highest) * inv_tau)
-                total = total + jnp.sum(terms.reshape(chunk // 8, 8, block_rows), axis=0)
-                coarse = terms.astype(jnp.bfloat16)
-                fine = (terms - coarse.astype(jnp.float32)).astype(jnp.bfloat16)
-                patch_rows = source[page, start : start + chunk]
-                mean = mean + contract(patch_rows, coarse, 0, 0) + contract(patch_rows, fine, 0, 0)
-            total = jnp.sum(total, axis=0, keepdims=True)
-            any_live = count > (slot - parity) * patch_local
-            smooth = highest + smooth_tau * (jnp.log(total) - log_row(count))
-            smooth = jnp.where(any_live, smooth, neg_large)
-            rows = jnp.transpose(mean / total)
+            count = integers[pl.ds(page, 1), :block_rows][:, :lanes]
+            running = jnp.full((block_rows, lanes), neg_large, jnp.float32)
+            for turn, (source, base) in enumerate(sources):
+                similar = contract(token_rows, source[page], 1, 1)
+                for place in places:
+                    live = position < count - base - place.start
+                    live = jnp.broadcast_to(live, (block_rows, lanes))
+                    masked = jnp.where(live, similar[:, place], neg_large)
+                    scores[turn, :, place] = masked
+                    running = jnp.maximum(running, masked)
+            highest = jnp.max(running, axis=1, keepdims=True)
+            total = jnp.zeros((block_rows, lanes), jnp.float32)
+            mean = jnp.zeros((block_rows, width), jnp.float32)
+            for turn, (source, base) in enumerate(sources):
+                coarse, fine = [], []
+                for place in places:
+                    terms = jnp.exp2((scores[turn, :, place] - highest) * inv_tau_log2)
+                    total = total + terms
+                    coarse.append(terms.astype(jnp.bfloat16))
+                    fine.append((terms - coarse[-1].astype(jnp.float32)).astype(jnp.bfloat16))
+                for part in (coarse, fine):
+                    mean = mean + contract(jnp.concatenate(part, axis=1), source[page], 1, 0)
+            total = jnp.sum(total, axis=1, keepdims=True)
+            mean = mean * (1.0 / total)
             for i in range(block_peers):
                 line = (b * block_peers + i) * lines + index * share
-                out[pl.ds(line, share)] = rows[i * share : (i + 1) * share]
-            for half in range(halves):
-                line = pair_pages * share + (b * pair_pages + index) * halves + half
-                part = smooth[:, half * lanes : (half + 1) * lanes]
-                out[pl.ds(line, peers, stride=lines)] = jnp.broadcast_to(part, (peers, lanes))
+                out[pl.ds(line, share)] = mean[i * share : (i + 1) * share]
+            any_live = count > (slot - parity) * patch_local
+            log_count = jnp.log(count.astype(jnp.float32))
+            for half in range(block_rows // lanes):
+                rows = slice(half * lanes, (half + 1) * lanes)
+                log_mean = jnp.log(as_row(total[rows])) - log_count
+                smooth = as_row(highest[rows]) + smooth_tau * log_mean
+                smooth = jnp.where(any_live, smooth, neg_large)
+                line = pair_pages * share + (b * pair_pages + index) * (block_rows // lanes) + half
+                out[pl.ds(line, peers, stride=lines)] = jnp.broadcast_to(smooth, (peers, lanes))
 
     over_blocks(tokens.shape[0] * tokens.shape[1] // block_rows, block)
 
@@ -161,7 +168,7 @@
                     for side in range(sides)
                 ]
                 highest = functools.reduce(jnp.maximum, heights)
-                terms = [jnp.exp((x - highest) * inv_tau) for x in heights]
+                terms = [jnp.exp2((x - highest) * inv_tau_log2) for x in heights]
                 total = functools.reduce(jnp.add, terms)
                 smooth.append(highest + smooth_tau * jnp.log(total))
                 parts.append([x / total for x in terms])
@@ -197,30 +204,42 @@
             page_lse = jnp.concatenate(row_lse[page], axis=1) + smooth_tau * log_row(count)
             for start in range(0, patch_local, chunk):
                 similar = contract(own[page, start : start + chunk], token_rows, 1, 1)
-                coef = page_weight * jnp.exp((similar - page_lse) * inv_tau)
+                coef = page_weight * jnp.exp2((similar - page_lse) * inv_tau_log2)
                 coef = jnp.where(position < live_count - start, coef, 0.0).astype(jnp.bfloat16)
                 grad = contract(coef, token_rows, 1, 0)
                 if tokens.shape[0] > block_queries:
                     grad = grad + jnp.where(b == 0, 0.0, page_grad[page, start : start + chunk])
                 page_grad[page, start : start + chunk] = grad
 
-        @pl.when(group // block_queries == b)
-        def _():
+        def own_rows():
             row = lax.rem(group, block_queries) * query_len + slot * share
-            half = row // lanes
-            grad = jnp.zeros((share, width), jnp.float32)
+            picked = []
             for page in pages:
                 for side in range(sides):
-                    picked = shares[0][page][side]
+                    x = shares[0][page][side]
                     for other in range(1, halves):
-                        picked = jnp.where(half == other, shares[other][page][side], picked)
-                    picked = pltpu.roll(picked, lax.rem(lanes - lax.rem(row, lanes), lanes), 1)
-                    columns = jnp.transpose(picked)[:share]
-                    for g in range(groups):
-                        line = (g * slots + sender(page, side)) * lines
-                        line = line + page % pair_pages * share
-                        grad = grad + columns[:, g : g + 1] * heard[line : line + share]
-            query_grad[0] = grad
+                        x = jnp.where(row // lanes == other, shares[other][page][side], x)
+                    picked.append(x)
+            picked = jnp.concatenate(picked, axis=0)
+            picked = pltpu.roll(picked, lax.rem(lanes - lax.rem(row, lanes), lanes), 1)
+            columns = jnp.transpose(picked)[:share]
+            grads = []
+            for page in pages:
+                for side in range(sides):
+                    place = len(grads) * groups
+                    first = sender(page, side) * lines + page % pair_pages * share
+                    terms = [
+                        columns[:, place + g : place + g + 1]
+                        * heard[first + g * slots * lines : first + g * slots * lines + share]
+                        for g in range(groups)
+                    ]
+                    grads.append(functools.reduce(jnp.add, terms))
+            query_grad[0] = functools.reduce(jnp.add, grads)
+
+        if tokens.shape[0] == block_queries:
+            own_rows()
+        else:
+            pl.when(group // block_queries == b)(own_rows)
 
     over_blocks(tokens.shape[0] // block_queries, block)
 
@@ -250,7 +269,7 @@
         ),
         in_specs=[vmem] * 5,
         out_specs=(vmem, vmem),
-        scratch_shapes=[pltpu.VMEM((2 * patch_local, block_rows), jnp.float32)],
+        scratch_shapes=[pltpu.VMEM((2, block_rows, patch_local), jnp.float32)],
         compiler_params=params,
         name="forward",
     )(patch_counts, positive_page, tokens, page_patches, partner)

time: 29 us -> 28.4 us (0.979)
  Pallas kernels: 2.73 us -> 2.17 us
    pallas_call x1, Pallas kernels: 1.05 us -> 0.74 us  [shards(): pl.pallas_call(functools.partial(forward_kernel, share, lines), out_shape...]
  transfers between devices with their start and end apart: 1 -> 1, of which waited for: 0 -> 0; matrix products, arithmetic and copies ran while one was open for 2% -> 3% of each run, Pallas kernels for 0% -> 0%
where the time goes in v3:
time: 28.4 us; the launch traced here: 28.2 us
  blocking collectives  24.1 us (85%)
  Pallas kernels  2.17 us (8%)
  local copies, waits for them, and re-layouts  0.72 us (3%)
  between operations  0.68 us (2%)
  starting transfers between devices  0.52 us (2%)
    all_to_all x1, blocking collectives, shards(): lax.all_to_all(jnp.broadcast_to(query_tokens, (page_groups, query_len, wi...  13.5 us
    all_to_all x1, blocking collectives, shards(): lax.all_to_all(told, both, 0, 0, tiled=True).reshape(peers * lines, lanes)  10.5 us
    pallas_call x1, Pallas kernels, shards(): pl.pallas_call(functools.partial(backward_kernel, slots, share, lines), o...  1.43 us
    pallas_call x1, Pallas kernels, shards(): pl.pallas_call(functools.partial(forward_kernel, share, lines), out_shape...  0.74 us
    broadcast_in_dim x1, local copies, waits for them, and re-layouts, shards(): jnp.broadcast_to(query_tokens, (page_groups, query_len, width))  0.71 us
  transfers between devices with their start and end apart: 1, of which 0 were waited for; matrix products, arithmetic and copies ran while one was open for 3% of the time, Pallas kernels for 0%

profile of v3, /device:TPU:0, one launch (start us, length us, event | category | flops | bytes accessed | tf_op | source)
XLA Modules:
  0.0 28.2 jit_solution(11344215914069303139)
XLA Ops:
  0.6 0.0 copy-start
  0.6 0.5 %collective-permute-start = (bf16[2,384,128]{2,1,0:T(8,128)(2,1)}, bf16[2,384,128]{2,1,0:T(8,128)(2,1)S(1)}, u32[]{:S(2)}, u32[]{:S(2)}) collective-permute-start(bf16[2,384,128]{2,1,0:T(8,128)(2,1)} %own.3), channel_id=1, source_target_pairs={{0,1},{1,0},{2,3},{3,2},{4,5},{5,4},{6,7},{7,6},{8,9},{9,8},{10,11... | collective-permute-start | bytes 589832 | tf_op jit(solution)/shard_map/ppermute | solution.py:260
  1.2 0.7 %broadcast_in_dim.8 = bf16[8,32,128]{2,1,0:T(8,128)(2,1)S(1)} broadcast(bf16[32,128]{1,0:T(8,128)(2,1)} %bitcast.5), dimensions={1,2} | broadcast | bytes 73728 | tf_op jit(solution)/shard_map/broadcast_in_dim | solution.py:262
  1.9 0.0 copy-start.1
  1.9 0.0 copy-start.2
  1.9 13.5 %all_to_all.10.tokens = bf16[8,32,128]{2,1,0:T(8,128)(2,1)S(1)} all-to-all(bf16[8,32,128]{2,1,0:T(8,128)(2,1)S(1)} %broadcast_in_dim.8), channel_id=1, replica_groups=mesh['pages'=8,'queries'=4] {'pages'}, dimensions={0} | all-to-all | bytes 131072 | tf_op jit(solution)/shard_map/all_to_all | solution.py:261
  15.4 0.0 collective-permute-done.partner
  15.4 0.0 copy-done
  15.4 0.0 copy-done.1
  15.4 0.0 copy-done.2
  15.5 0.7 %forward.1 = (f32[320,128]{1,0:T(8,128)S(1)}, s32[3,256]{1,0:T(4,128)S(1)}) custom-call(s32[2]{0:T(128)S(1)} %copy-done.1, s32[8]{0:T(128)S(1)} %copy-done.2, bf16[8,32,128]{2,1,0:T(8,128)(2,1)S(1)} %all_to_all.10.tokens, bf16[2,384,128]{2,1,0:T(8,128)(2,1)S(1)} %copy-done, bf16[2,384,128]{2,1,0:T(8,128)(2,1)S(1)} %collective-permute-done.partner), custom_call_target="tpu_custom_call" | custom-call | tf_op jit(solution)/shard_map/forward/pallas_call | solution.py:264
  16.2 10.5 %all_to_all.11 = f32[32,5,2,128]{3,2,1,0:T(2,128)S(1)} all-to-all(f32[32,5,2,128]{3,2,1,0:T(2,128)S(1)} %bitcast.4), channel_id=1, replica_groups=mesh['pages'=8,'queries'=4] {'pages','queries'}, dimensions={0} | all-to-all | bytes 327680 | tf_op jit(solution)/shard_map/all_to_all | solution.py:277
  26.7 1.4 %backward.1 = (f32[8]{0:T(128)}, f32[1,8,128]{2,1,0:T(8,128)}, f32[2,384,128]{2,1,0:T(8,128)}) custom-call(s32[3,256]{1,0:T(4,128)S(1)} %get-tuple-element.5.integers, f32[320,128]{1,0:T(8,128)S(1)} %bitcast.3, bf16[8,32,128]{2,1,0:T(8,128)(2,1)S(1)} %all_to_all.10.tokens, bf16[2,384,128]{2,1,0:T(8,128)(2,1)S(1)} %copy-done), custom_call_target="tpu_custom_call" | custom-call | tf_op jit(solution)/shard_map/backward/pallas_call | solution.py:278
Async XLA Ops:
  0.6 14.8 %copy-start = (bf16[2,384,128]{2,1,0:T(8,128)(2,1)S(1)}, bf16[2,384,128]{2,1,0:T(8,128)(2,1)}, u32[]{:S(2)}) copy-start(bf16[2,384,128]{2,1,0:T(8,128)(2,1)} %own.3) | copy-start | bytes 589828
  0.6 14.8 %collective-permute-start = (bf16[2,384,128]{2,1,0:T(8,128)(2,1)}, bf16[2,384,128]{2,1,0:T(8,128)(2,1)S(1)}, u32[]{:S(2)}, u32[]{:S(2)}) collective-permute-start(bf16[2,384,128]{2,1,0:T(8,128)(2,1)} %own.3), channel_id=1, source_target_pairs={{0,1},{1,0},{2,3},{3,2},{4,5},{5,4},{6,7},{7,6},{8,9},{9,8},{10,11... | collective-permute-start | bytes 589832 | tf_op jit(solution)/shard_map/ppermute | solution.py:260
  1.9 13.6 %copy-start.1 = (s32[2]{0:T(128)S(1)}, s32[2]{0:T(128)}, u32[]{:S(2)}) copy-start(s32[2]{0:T(128)} %counts.1) | copy-start | bytes 28
  1.9 13.6 %copy-start.2 = (s32[8]{0:T(128)S(1)}, s32[8]{0:T(128)}, u32[]{:S(2)}) copy-start(s32[8]{0:T(128)} %positive.1) | copy-start | bytes 100

commit v4 on v3

--- a/solution.py
+++ b/solution.py
@@ -18,6 +18,7 @@
 block_rows = 256
 chunk = 128
 both = ("pages", "queries")
+fetches = ((6, 7, 2, 0), (5, 3, 1, 4))
 
 
 def contract(a, b, dim_a, dim_b):
@@ -39,24 +40,51 @@
     return tokens[pl.ds(start, count)].reshape(block_rows, tokens.shape[2])
 
 
-def integer_rows(counts, positive, rows):
+def log_row(count):
+    return jnp.log(count.astype(jnp.float32))
+
+
+def integer_rows(counts, positive, integers):
     counts, positive = counts[...][None], positive[...][None]
-    lists = [jnp.broadcast_to(counts[:, i : i + 1], (1, rows)) for i in range(counts.shape[1])]
+    page_local = counts.shape[1]
+    rows = integers.shape[1]
+    for page in range(page_local):
+        integers[page : page + 1] = jnp.broadcast_to(counts[:, page : page + 1], (1, rows))
     query_count = positive.shape[1]
     row_query = lax.broadcasted_iota(jnp.int32, (1, rows), 1) // (rows // query_count)
     target = jnp.zeros((1, rows), jnp.int32)
     for query in range(query_count):
         target = jnp.where(row_query == query, positive[:, query : query + 1], target)
-    return jnp.concatenate([*lists, target], axis=0)
-
-
-def log_row(count):
-    return jnp.log(count.astype(jnp.float32))
-
-
-def forward_kernel(
-    share, lines, counts, positive, tokens, own, partner, out, integers, scores
-):
+    integers[page_local : page_local + 1] = target
+
+
+def hold_kernel(patches, out):
+    out[...] = patches[...]
+
+
+def gather_kernel(counts, positive, _, tokens, *refs):
+    fetched, (gathered, mine, integers) = refs[:-3], refs[-3:]
+    integer_rows(counts, positive, integers)
+    mine[...] = tokens[...]
+    for i, ref in enumerate(fetched):
+        gathered[i] = ref[0]
+
+
+def assembled_kernel(share, lines, integers, own, partner, mine, *refs):
+    slots = len(fetches[0])
+    fetched, others, (out, tokens, scores) = refs[:slots], refs[slots], refs[slots + 1 :]
+    group = lax.axis_index("pages")
+    parity = lax.rem(lax.axis_index("queries"), 2)
+    tokens[pl.ds(group, 1)] = mine[...]
+    for side in range(2):
+        for i, shift in enumerate(fetches[side]):
+            if shift:
+                block = jnp.where(parity == side, fetched[i][...], others[i : i + 1])
+                tokens[pl.ds(group ^ shift, 1)] = block
+    forward_kernel(share, lines, integers, tokens, own, partner, out, scores)
+
+
+def forward_kernel(share, lines, integers, tokens, own, partner, out, scores):
     page_local, patch_local, width = own.shape
     block_peers = block_rows // share
     peers = out.shape[0] // lines
@@ -69,7 +97,6 @@
         jnp.int32, (lanes, lanes), 1
     )
     places = [slice(start, start + lanes) for start in range(0, patch_local, lanes)]
-    integers[...] = integer_rows(counts, positive, integers.shape[1])
 
     def as_row(column):
         return jnp.sum(jnp.where(diagonal, column, 0.0), axis=0, keepdims=True)
@@ -244,6 +271,15 @@
     over_blocks(tokens.shape[0] // block_queries, block)
 
 
+def fetch_pairs(page_groups, slots, shifts):
+    return [
+        (group * slots + slot, (group ^ shifts[slot % 2]) * slots + slot)
+        for group in range(page_groups)
+        for slot in range(slots)
+        if shifts[slot % 2]
+    ]
+
+
 def shards(page_groups, slots, query_tokens, page_patches, patch_counts, positive_page):
     query_local, query_len, width = query_tokens.shape
     page_local, patch_local, _ = page_patches.shape
@@ -258,21 +294,69 @@
     params = pltpu.CompilerParams(vmem_limit_bytes=limit)
 
     partner = lax.ppermute(page_patches, "queries", [(i, i ^ 1) for i in range(slots)])
-    tokens = lax.all_to_all(
-        jnp.broadcast_to(query_tokens, (page_groups, query_len, width)), "pages", 0, 0, tiled=True
-    )
-    told, integers = pl.pallas_call(
-        functools.partial(forward_kernel, share, lines),
-        out_shape=(
-            jax.ShapeDtypeStruct((peers * lines, lanes), jnp.float32),
-            jax.ShapeDtypeStruct((page_local + 1, query_count * query_len), jnp.int32),
-        ),
-        in_specs=[vmem] * 5,
-        out_specs=(vmem, vmem),
-        scratch_shapes=[pltpu.VMEM((2, block_rows, patch_local), jnp.float32)],
-        compiler_params=params,
-        name="forward",
-    )(patch_counts, positive_page, tokens, page_patches, partner)
+    token_shape = jax.ShapeDtypeStruct((page_groups, query_len, width), query_tokens.dtype)
+    told_shape = jax.ShapeDtypeStruct((peers * lines, lanes), jnp.float32)
+    scores = pltpu.VMEM((2, block_rows, patch_local), jnp.float32)
+    small = pltpu.CompilerParams(vmem_limit_bytes=4 << 20)
+    integer_shape = jax.ShapeDtypeStruct((page_local + 1, query_count * query_len), jnp.int32)
+    if page_groups == 1 + sum(1 for side in fetches for shift in side if shift):
+        fetched = [
+            lax.ppermute(query_tokens, both, fetch_pairs(page_groups, slots, shifts))
+            for shifts in zip(*fetches)
+        ]
+        held = pl.pallas_call(
+            hold_kernel,
+            out_shape=jax.ShapeDtypeStruct(page_patches.shape, page_patches.dtype),
+            in_specs=[vmem],
+            out_specs=vmem,
+            compiler_params=small,
+            cost_estimate=pl.CostEstimate(flops=0, bytes_accessed=1 << 24, transcendentals=0),
+            name="hold",
+        )(page_patches)
+        gathered, mine, integers = pl.pallas_call(
+            gather_kernel,
+            out_shape=(
+                jax.ShapeDtypeStruct((len(fetched), query_len, width), query_tokens.dtype),
+                jax.ShapeDtypeStruct(query_tokens.shape, query_tokens.dtype),
+                integer_shape,
+            ),
+            in_specs=[vmem] * (len(fetched) + 4),
+            out_specs=(vmem, vmem, vmem),
+            compiler_params=small,
+            name="gather",
+        )(patch_counts, positive_page, held, query_tokens, *fetched)
+        others = lax.ppermute(gathered, "queries", [(i, i ^ 1) for i in range(slots)])
+        told, tokens = pl.pallas_call(
+            functools.partial(assembled_kernel, share, lines),
+            out_shape=(told_shape, token_shape),
+            in_specs=[vmem] * (5 + len(fetched)),
+            out_specs=(vmem, vmem),
+            scratch_shapes=[scores],
+            compiler_params=params,
+            name="forward",
+        )(integers, held, partner, mine, *fetched, others)
+    else:
+        tokens = lax.all_to_all(
+            jnp.broadcast_to(query_tokens, token_shape.shape), "pages", 0, 0, tiled=True
+        )
+        held = page_patches
+        integers = pl.pallas_call(
+            integer_rows,
+            out_shape=integer_shape,
+            in_specs=[vmem] * 2,
+            out_specs=vmem,
+            compiler_params=small,
+            name="integers",
+        )(patch_counts, positive_page)
+        told = pl.pallas_call(
+            functools.partial(forward_kernel, share, lines),
+            out_shape=told_shape,
+            in_specs=[vmem] * 4,
+            out_specs=vmem,
+            scratch_shapes=[scores],
+            compiler_params=params,
+            name="forward",
+        )(integers, tokens, held, partner)
     told = told.reshape(peers, lines // tile, tile, lanes)
     heard = lax.all_to_all(told, both, 0, 0, tiled=True).reshape(peers * lines, lanes)
     return pl.pallas_call(
@@ -286,7 +370,7 @@
         out_specs=(smem, vmem, vmem),
         compiler_params=params,
         name="backward",
-    )(integers, heard, tokens, page_patches)
+    )(integers, heard, tokens, held)
 
 
 def solution(mesh):

time: 28.4 us -> 27.7 us (0.975)
  blocking collectives: 24.1 us -> 10.4 us
  starting transfers between devices: 0.52 us -> 9.62 us
  waiting for transfers between devices: 0.01 us -> 3.56 us
    all_to_all x1 -> x0, blocking collectives: 13.5 us -> none  [shards(): lax.all_to_all(jnp.broadcast_to(query_tokens, (page_groups, query_len, wi...]
    ppermute x0 -> x5, starting transfers between devices: none -> 9.11 us  [the longest x4 8.05 us: shards(): lax.ppermute(query_tokens, both, fetch_pairs(page_groups, slots, shifts))]
    ppermute x0 -> x5, waiting for transfers between devices: none -> 3.56 us  [the longest x4 2.7 us: shards(): lax.ppermute(query_tokens, both, fetch_pairs(page_groups, slots, shifts))]
    unnamed x6 -> x8, local copies, waits for them, and re-layouts: 0.02 us -> 0.93 us
    broadcast_in_dim x1 -> x0, local copies, waits for them, and re-layouts: 0.71 us -> none  [shards(): jnp.broadcast_to(query_tokens, (page_groups, query_len, width))]
    pallas_call x1 -> x3, Pallas kernels: 0.74 us -> 0.84 us  [the longest x1 0.74 us: shards(): pl.pallas_call(functools.partial(assembled_kernel, share, lines), out_sha...]
  transfers between devices with their start and end apart: 1 -> 6, of which waited for: 0 -> 3; matrix products, arithmetic and copies ran while one was open for 3% -> 0% of each run, Pallas kernels for 0% -> 0%
where the time goes in v4:
time: 27.7 us; the launch traced here: 27.5 us
  blocking collectives  10.4 us (38%)
  starting transfers between devices  9.62 us (35%)
  waiting for transfers between devices  3.56 us (13%)
  Pallas kernels  2.26 us (8%)
  local copies, waits for them, and re-layouts  0.93 us (3%)
  between operations  0.69 us (2%)
    all_to_all x1, blocking collectives, shards(): lax.all_to_all(told, both, 0, 0, tiled=True).reshape(peers * lines, lanes)  10.4 us
    ppermute x4, starting transfers between devices, shards(): lax.ppermute(query_tokens, both, fetch_pairs(page_groups, slots, shifts))  8.05 us
    ppermute x4, waiting for transfers between devices, shards(): lax.ppermute(query_tokens, both, fetch_pairs(page_groups, slots, shifts))  2.7 us
    pallas_call x1, Pallas kernels, shards(): pl.pallas_call(functools.partial(backward_kernel, slots, share, lines), o...  1.43 us
    ppermute x1, starting transfers between devices, shards(): lax.ppermute(gathered, 'queries', [(i, i ^ 1) for i in range(slots)])  1.06 us
    unnamed x8, local copies, waits for them, and re-layouts  0.93 us
    ppermute x1, waiting for transfers between devices, shards(): lax.ppermute(gathered, 'queries', [(i, i ^ 1) for i in range(slots)])  0.86 us
    pallas_call x1, Pallas kernels, shards(): pl.pallas_call(functools.partial(assembled_kernel, share, lines), out_sha...  0.74 us
  transfers between devices with their start and end apart: 6, of which 3 were waited for; matrix products, arithmetic and copies ran while one was open for 0% of the time, Pallas kernels for 0%

profile of v4, /device:TPU:0, one launch (start us, length us, event | category | flops | bytes accessed | tf_op | source)
XLA Modules:
  0.0 27.5 jit_solution(9857017087719279398)
XLA Ops:
  0.6 0.5 %collective-permute-start.4 = (bf16[2,384,128]{2,1,0:T(8,128)(2,1)}, bf16[2,384,128]{2,1,0:T(8,128)(2,1)S(1)}, u32[]{:S(2)}, u32[]{:S(2)}) collective-permute-start(bf16[2,384,128]{2,1,0:T(8,128)(2,1)} %patches.1), channel_id=1, source_target_pairs={{0,1},{1,0},{2,3},{3,2},{4,5},{5,4},{6,7},{7,6},{8,9},{9,8},{10,11... | collective-permute-start | bytes 589832 | tf_op jit(solution)/shard_map/ppermute | solution.py:296
  1.1 2.6 %collective-permute-start.2 = (bf16[1,32,128]{2,1,0:T(8,128)(2,1)}, bf16[1,32,128]{2,1,0:T(8,128)(2,1)S(1)}, u32[]{:S(2)}, u32[]{:S(2)}) collective-permute-start(bf16[1,32,128]{2,1,0:T(8,128)(2,1)} %tokens.1), channel_id=1, source_target_pairs={{0,8},{1,5},{2,10},{3,7},{4,12},{5,1},{6,14},{7,3},{8,0},{9,13},{1... | collective-permute-start | bytes 24584 | tf_op jit(solution)/shard_map/ppermute | solution.py:304
  3.8 3.4 %collective-permute-start.1 = (bf16[1,32,128]{2,1,0:T(8,128)(2,1)}, bf16[1,32,128]{2,1,0:T(8,128)(2,1)S(1)}, u32[]{:S(2)}, u32[]{:S(2)}) collective-permute-start(bf16[1,32,128]{2,1,0:T(8,128)(2,1)} %tokens.1), channel_id=1, source_target_pairs={{0,28},{1,13},{2,30},{3,15},{4,24},{5,9},{6,26},{7,11},{8,20},{9,5... | collective-permute-start | bytes 24584 | tf_op jit(solution)/shard_map/ppermute | solution.py:304
  7.2 1.3 %collective-permute-start = (bf16[1,32,128]{2,1,0:T(8,128)(2,1)}, bf16[1,32,128]{2,1,0:T(8,128)(2,1)S(1)}, u32[]{:S(2)}, u32[]{:S(2)}) collective-permute-start(bf16[1,32,128]{2,1,0:T(8,128)(2,1)} %tokens.1), channel_id=1, source_target_pairs={{0,24},{1,21},{2,26},{3,23},{4,28},{5,17},{6,30},{7,19},{8,16},{9,... | collective-permute-start | bytes 24584 | tf_op jit(solution)/shard_map/ppermute | solution.py:304
  8.6 0.6 %collective-permute-start.3 = (bf16[1,32,128]{2,1,0:T(8,128)(2,1)}, bf16[1,32,128]{2,1,0:T(8,128)(2,1)S(1)}, u32[]{:S(2)}, u32[]{:S(2)}) collective-permute-start(bf16[1,32,128]{2,1,0:T(8,128)(2,1)} %tokens.1), channel_id=1, source_target_pairs={{1,17},{3,19},{5,21},{7,23},{9,25},{11,27},{13,29},{15,31},{17,1},... | collective-permute-start | bytes 24584 | tf_op jit(solution)/shard_map/ppermute | solution.py:304
  9.2 0.0 copy-start
  9.2 0.9 %copy-done = bf16[2,384,128]{2,1,0:T(8,128)(2,1)S(1)} copy-done((bf16[2,384,128]{2,1,0:T(8,128)(2,1)S(1)}, bf16[2,384,128]{2,1,0:T(8,128)(2,1)}, u32[]{:S(2)}) %copy-start) | copy-done | bytes 196632
  10.1 0.0 copy-start.1
  10.1 0.0 copy-start.2
  10.1 0.0 copy-start.3
  10.2 0.0 collective-permute-done.2.refs_2_
  10.2 0.2 collective-permute-done.1.refs_1_
  10.4 2.5 %collective-permute-done.refs_0_ = bf16[1,32,128]{2,1,0:T(8,128)(2,1)S(1)} collective-permute-done((bf16[1,32,128]{2,1,0:T(8,128)(2,1)}, bf16[1,32,128]{2,1,0:T(8,128)(2,1)S(1)}, u32[]{:S(2)}, u32[]{:S(2)}) %collective-permute-start) | collective-permute-done | bytes 8224 | tf_op jit(solution)/shard_map/ppermute | solution.py:304
  12.9 0.0 collective-permute-done.3.refs_3_
  12.9 0.0 copy-done.1
  12.9 0.0 copy-done.2
  12.9 0.0 copy-done.3
  12.9 0.1 gather.1
  13.0 1.1 %collective-permute-start.5 = (bf16[4,32,128]{2,1,0:T(8,128)(2,1)S(1)}, bf16[4,32,128]{2,1,0:T(8,128)(2,1)S(1)}, u32[]{:S(2)}, u32[]{:S(2)}) collective-permute-start(bf16[4,32,128]{2,1,0:T(8,128)(2,1)S(1)} %get-tuple-element.10), channel_id=1, source_target_pairs={{0,1},{1,0},{2,3},{3,2},{4,5},{5,4},{6,7},{7,6},{8,9},{9,8},{10,11... | collective-permute-start | bytes 98312 | tf_op jit(solution)/shard_map/ppermute | solution.py:328
  14.0 0.9 %collective-permute-done.5.refs_4_ = bf16[4,32,128]{2,1,0:T(8,128)(2,1)S(1)} collective-permute-done((bf16[4,32,128]{2,1,0:T(8,128)(2,1)S(1)}, bf16[4,32,128]{2,1,0:T(8,128)(2,1)S(1)}, u32[]{:S(2)}, u32[]{:S(2)}) %collective-permute-start.5) | collective-permute-done | bytes 32800 | tf_op jit(solution)/shard_map/ppermute | solution.py:328
  14.9 0.0 collective-permute-done.4.partner
  14.9 0.7 %forward.1 = (f32[320,128]{1,0:T(8,128)S(1)}, bf16[8,32,128]{2,1,0:T(8,128)(2,1)S(1)}) custom-call(s32[3,256]{1,0:T(4,128)S(1)} %get-tuple-element.8.integers, bf16[2,384,128]{2,1,0:T(8,128)(2,1)S(1)} %hold.1._.own, bf16[2,384,128]{2,1,0:T(8,128)(2,1)S(1)} %collective-permute-done.4.partner, bf16[1,32,128]{2,1,0:T(8,128)(2,1)S(1)} %get-tuple-element.9.mine, ...), custom_call_target="tpu_custom_call" | custom-call | tf_op jit(solution)/shard_map/forward/pallas_call | solution.py:329
  15.6 10.4 %all_to_all.5 = f32[32,5,2,128]{3,2,1,0:T(2,128)S(1)} all-to-all(f32[32,5,2,128]{3,2,1,0:T(2,128)S(1)} %bitcast.3), channel_id=1, replica_groups=mesh['pages'=8,'queries'=4] {'pages','queries'}, dimensions={0} | all-to-all | bytes 327680 | tf_op jit(solution)/shard_map/all_to_all | solution.py:361
  26.0 1.4 %backward.1 = (f32[8]{0:T(128)}, f32[1,8,128]{2,1,0:T(8,128)}, f32[2,384,128]{2,1,0:T(8,128)}) custom-call(s32[3,256]{1,0:T(4,128)S(1)} %get-tuple-element.8.integers, f32[320,128]{1,0:T(8,128)S(1)} %bitcast.2, bf16[8,32,128]{2,1,0:T(8,128)(2,1)S(1)} %get-tuple-element.12.tokens, bf16[2,384,128]{2,1,0:T(8,128)(2,1)S(1)} %hold.1._.own), custom_call_target="tpu_custom_call" | custom-call | tf_op jit(solution)/shard_map/backward/pallas_call | solution.py:362
  (1 shorter events, 0.0 us)
Async XLA Ops:
  0.6 14.3 %collective-permute-start.4 = (bf16[2,384,128]{2,1,0:T(8,128)(2,1)}, bf16[2,384,128]{2,1,0:T(8,128)(2,1)S(1)}, u32[]{:S(2)}, u32[]{:S(2)}) collective-permute-start(bf16[2,384,128]{2,1,0:T(8,128)(2,1)} %patches.1), channel_id=1, source_target_pairs={{0,1},{1,0},{2,3},{3,2},{4,5},{5,4},{6,7},{7,6},{8,9},{9,8},{10,11... | collective-permute-start | bytes 589832 | tf_op jit(solution)/shard_map/ppermute | solution.py:296
  1.1 9.0 %collective-permute-start.2 = (bf16[1,32,128]{2,1,0:T(8,128)(2,1)}, bf16[1,32,128]{2,1,0:T(8,128)(2,1)S(1)}, u32[]{:S(2)}, u32[]{:S(2)}) collective-permute-start(bf16[1,32,128]{2,1,0:T(8,128)(2,1)} %tokens.1), channel_id=1, source_target_pairs={{0,8},{1,5},{2,10},{3,7},{4,12},{5,1},{6,14},{7,3},{8,0},{9,13},{1... | collective-permute-start | bytes 24584 | tf_op jit(solution)/shard_map/ppermute | solution.py:304
  3.8 6.6 %collective-permute-start.1 = (bf16[1,32,128]{2,1,0:T(8,128)(2,1)}, bf16[1,32,128]{2,1,0:T(8,128)(2,1)S(1)}, u32[]{:S(2)}, u32[]{:S(2)}) collective-permute-start(bf16[1,32,128]{2,1,0:T(8,128)(2,1)} %tokens.1), channel_id=1, source_target_pairs={{0,28},{1,13},{2,30},{3,15},{4,24},{5,9},{6,26},{7,11},{8,20},{9,5... | collective-permute-start | bytes 24584 | tf_op jit(solution)/shard_map/ppermute | solution.py:304
  7.2 5.7 %collective-permute-start = (bf16[1,32,128]{2,1,0:T(8,128)(2,1)}, bf16[1,32,128]{2,1,0:T(8,128)(2,1)S(1)}, u32[]{:S(2)}, u32[]{:S(2)}) collective-permute-start(bf16[1,32,128]{2,1,0:T(8,128)(2,1)} %tokens.1), channel_id=1, source_target_pairs={{0,24},{1,21},{2,26},{3,23},{4,28},{5,17},{6,30},{7,19},{8,16},{9,... | collective-permute-start | bytes 24584 | tf_op jit(solution)/shard_map/ppermute | solution.py:304
  8.6 4.3 %collective-permute-start.3 = (bf16[1,32,128]{2,1,0:T(8,128)(2,1)}, bf16[1,32,128]{2,1,0:T(8,128)(2,1)S(1)}, u32[]{:S(2)}, u32[]{:S(2)}) collective-permute-start(bf16[1,32,128]{2,1,0:T(8,128)(2,1)} %tokens.1), channel_id=1, source_target_pairs={{1,17},{3,19},{5,21},{7,23},{9,25},{11,27},{13,29},{15,31},{17,1},... | collective-permute-start | bytes 24584 | tf_op jit(solution)/shard_map/ppermute | solution.py:304
  9.2 0.9 %copy-start = (bf16[2,384,128]{2,1,0:T(8,128)(2,1)S(1)}, bf16[2,384,128]{2,1,0:T(8,128)(2,1)}, u32[]{:S(2)}) copy-start(bf16[2,384,128]{2,1,0:T(8,128)(2,1)} %patches.1) | copy-start | bytes 589828
  10.1 2.7 %copy-start.1 = (bf16[1,32,128]{2,1,0:T(8,128)(2,1)S(1)}, bf16[1,32,128]{2,1,0:T(8,128)(2,1)}, u32[]{:S(2)}) copy-start(bf16[1,32,128]{2,1,0:T(8,128)(2,1)} %tokens.1) | copy-start | bytes 24580
  10.1 2.7 %copy-start.2 = (s32[2]{0:T(128)S(1)}, s32[2]{0:T(128)}, u32[]{:S(2)}) copy-start(s32[2]{0:T(128)} %counts.1) | copy-start | bytes 28
  10.1 2.7 %copy-start.3 = (s32[8]{0:T(128)S(1)}, s32[8]{0:T(128)}, u32[]{:S(2)}) copy-start(s32[8]{0:T(128)} %positive.1) | copy-start | bytes 100
  13.0 1.9 %collective-permute-start.5 = (bf16[4,32,128]{2,1,0:T(8,128)(2,1)S(1)}, bf16[4,32,128]{2,1,0:T(8,128)(2,1)S(1)}, u32[]{:S(2)}, u32[]{:S(2)}) collective-permute-start(bf16[4,32,128]{2,1,0:T(8,128)(2,1)S(1)} %get-tuple-element.10), channel_id=1, source_target_pairs={{0,1},{1,0},{2,3},{3,2},{4,5},{5,4},{6,7},{7,6},{8,9},{9,8},{10,11... | collective-permute-start | bytes 98312 | tf_op jit(solution)/shard_map/ppermute | solution.py:328

commit v5 on v4

--- a/solution.py
+++ b/solution.py
@@ -16,9 +16,8 @@
 inv_tau_log2 = inv_tau / math.log(2.0)
 lanes = 128
 block_rows = 256
-chunk = 128
 both = ("pages", "queries")
-fetches = ((6, 7, 2, 0), (5, 3, 1, 4))
+fetches = ((6, 7, 2), (5, 1, 3, 4))
 
 
 def contract(a, b, dim_a, dim_b):
@@ -62,41 +61,136 @@
     out[...] = patches[...]
 
 
-def gather_kernel(counts, positive, _, tokens, *refs):
-    fetched, (gathered, mine, integers) = refs[:-3], refs[-3:]
+def gather_kernel(_, *refs):
+    for i, ref in enumerate(refs[:-1]):
+        refs[-1][i] = ref[0]
+
+
+def pair_patches(own, partner):
+    slot = lax.axis_index("queries")
+    parity = lax.rem(slot, 2)
+    patch_local = own.shape[1]
+    sources = ((own, slot * patch_local), (partner, (slot + 1 - 2 * parity) * patch_local))
+    return sources, parity, (slot - parity) * patch_local
+
+
+def page_softmax(token_rows, sources, page, count, scores):
+    rows = token_rows.shape[0]
+    _, patch_local, width = sources[0][0].shape
+    position = lax.broadcasted_iota(jnp.int32, (1, lanes), 1)
+    places = [slice(start, start + lanes) for start in range(0, patch_local, lanes)]
+    running = jnp.full((rows, lanes), neg_large, jnp.float32)
+    for turn, (source, base) in enumerate(sources):
+        similar = contract(token_rows, source[page], 1, 1)
+        for place in places:
+            live = jnp.broadcast_to(position < count - base - place.start, (rows, lanes))
+            masked = jnp.where(live, similar[:, place], neg_large)
+            scores[turn, :, place] = masked
+            running = jnp.maximum(running, masked)
+    highest = jnp.max(running, axis=1, keepdims=True)
+    total = jnp.zeros((rows, lanes), jnp.float32)
+    mean = jnp.zeros((rows, width), jnp.float32)
+    for turn, (source, base) in enumerate(sources):
+        coarse, fine = [], []
+        for place in places:
+            terms = jnp.exp2((scores[turn, :, place] - highest) * inv_tau_log2)
+            total = total + terms
+            coarse.append(terms.astype(jnp.bfloat16))
+            fine.append((terms - coarse[-1].astype(jnp.float32)).astype(jnp.bfloat16))
+        halves = [jnp.concatenate(part, axis=1) for part in (coarse, fine)]
+        product = contract(jnp.concatenate(halves, axis=0), source[page], 1, 0)
+        mean = mean + product[:rows] + product[rows:]
+    total = jnp.sum(total, axis=1, keepdims=True)
+    return mean * (1.0 / total), highest, total
+
+
+def query_rows(columns, queries):
+    query_len = columns[0].shape[0] // len(queries)
+    per_row = lanes // query_len
+    lane = lax.broadcasted_iota(jnp.int32, (query_len, lanes), 1)
+    line = lax.broadcasted_iota(jnp.int32, (query_len, lanes), 0)
+    masks = [lane == line + lax.rem(query, per_row) * query_len for query in queries]
+    result = []
+    for column in columns:
+        rows = [jnp.zeros((1, lanes), jnp.float32) for _ in range(block_rows // lanes)]
+        for i, (query, mask) in enumerate(zip(queries, masks)):
+            part = jnp.where(mask, column[i * query_len : (i + 1) * query_len], 0.0)
+            part = jnp.sum(part, axis=0, keepdims=True)
+            rows = [
+                row + jnp.where(query // per_row == half, part, 0.0)
+                for half, row in enumerate(rows)
+            ]
+        result.append(jnp.concatenate(rows, axis=0))
+    return result
+
+
+def early_kernel(counts, positive, own, partner, mine, *refs):
+    fetched, (means, lines, integers, scores) = refs[:-4], refs[-4:]
     integer_rows(counts, positive, integers)
-    mine[...] = tokens[...]
-    for i, ref in enumerate(fetched):
-        gathered[i] = ref[0]
-
-
-def assembled_kernel(share, lines, integers, own, partner, mine, *refs):
-    slots = len(fetches[0])
-    fetched, others, (out, tokens, scores) = refs[:slots], refs[slots], refs[slots + 1 :]
+    sources, parity, _ = pair_patches(own, partner)
     group = lax.axis_index("pages")
-    parity = lax.rem(lax.axis_index("queries"), 2)
-    tokens[pl.ds(group, 1)] = mine[...]
-    for side in range(2):
-        for i, shift in enumerate(fetches[side]):
-            if shift:
-                block = jnp.where(parity == side, fetched[i][...], others[i : i + 1])
-                tokens[pl.ds(group ^ shift, 1)] = block
-    forward_kernel(share, lines, integers, tokens, own, partner, out, scores)
+    count = integers[pl.ds(parity, 1), :block_rows][:, :lanes]
+    blocks = [mine[0]] + [ref[0] for ref in fetched]
+    queries = [group] + [
+        group ^ jnp.where(parity == 0, first, second)
+        for first, second in zip(*[side[: len(fetched)] for side in fetches])
+    ]
+    mean, highest, total = page_softmax(
+        jnp.concatenate(blocks, axis=0), sources, parity, count, scores
+    )
+    means[...] = mean.reshape(means.shape)
+    for i, rows in enumerate(query_rows((highest, total), queries)):
+        lines[i] = rows
+
+
+def late_kernel(
+    share, integers, own, partner, early_means, early_lines, mine, *refs
+):
+    fetched, others, (out, tokens, scores) = refs[:-4], refs[-4], refs[-3:]
+    sources, parity, first_slot = pair_patches(own, partner)
+    group = lax.axis_index("pages")
+    count = integers[pl.ds(parity, 1), :block_rows][:, :lanes]
+    near = len(fetched) - 1
+    blocks = [jnp.where(parity == 1, fetched[near][0], others[near])]
+    blocks = blocks + [others[i] for i in range(near)]
+    early_blocks = [mine[0]] + [ref[0] for ref in fetched[:near]]
+    early_queries, queries = [group], [group ^ fetches[1][near]]
+    for first, second in zip(*[side[:near] for side in fetches]):
+        early_queries.append(group ^ jnp.where(parity == 0, first, second))
+        queries.append(group ^ jnp.where(parity == 0, second, first))
+    mean, highest, total = page_softmax(
+        jnp.concatenate(blocks, axis=0), sources, parity, count, scores
+    )
+    query_len = blocks[0].shape[0]
+    lines = out.shape[1] * share // query_len
+    for i, query in enumerate(queries):
+        tokens[pl.ds(query, 1)] = blocks[i][None]
+        tokens[pl.ds(early_queries[i], 1)] = early_blocks[i][None]
+        for k in range(query_len // share):
+            part = mean[i * query_len + k * share : i * query_len + (k + 1) * share]
+            place = (slice(k * lines, k * lines + share), slice(None))
+            out[(pl.ds(query, 1), *place)] = part[None]
+            part = early_means[i, k * share : (k + 1) * share]
+            out[(pl.ds(early_queries[i], 1), *place)] = part[None]
+    highest, total = query_rows((highest, total), queries)
+    highest, total = highest + early_lines[0], total + early_lines[1]
+    smooth = highest + smooth_tau * (jnp.log(total) - jnp.log(count.astype(jnp.float32)))
+    smooth = jnp.where(count > first_slot, smooth, neg_large)
+    peers = out.shape[0] * out.shape[1] // lines
+    flat = out.reshape(peers * lines, lanes)
+    for half in range(smooth.shape[0]):
+        row = jnp.broadcast_to(smooth[half : half + 1], (peers, lanes))
+        flat[pl.ds(share + half, peers, stride=lines)] = row
 
 
 def forward_kernel(share, lines, integers, tokens, own, partner, out, scores):
-    page_local, patch_local, width = own.shape
     block_peers = block_rows // share
     peers = out.shape[0] // lines
-    pair_pages = page_local // 2
-    slot = lax.axis_index("queries")
-    parity = lax.rem(slot, 2)
-    sources = ((own, slot * patch_local), (partner, (slot + 1 - 2 * parity) * patch_local))
-    position = lax.broadcasted_iota(jnp.int32, (1, lanes), 1)
+    pair_pages = own.shape[0] // 2
+    sources, parity, first_slot = pair_patches(own, partner)
     diagonal = lax.broadcasted_iota(jnp.int32, (lanes, lanes), 0) == lax.broadcasted_iota(
         jnp.int32, (lanes, lanes), 1
     )
-    places = [slice(start, start + lanes) for start in range(0, patch_local, lanes)]
 
     def as_row(column):
         return jnp.sum(jnp.where(diagonal, column, 0.0), axis=0, keepdims=True)
@@ -106,39 +200,16 @@
         for index in range(pair_pages):
             page = parity * pair_pages + index
             count = integers[pl.ds(page, 1), :block_rows][:, :lanes]
-            running = jnp.full((block_rows, lanes), neg_large, jnp.float32)
-            for turn, (source, base) in enumerate(sources):
-                similar = contract(token_rows, source[page], 1, 1)
-                for place in places:
-                    live = position < count - base - place.start
-                    live = jnp.broadcast_to(live, (block_rows, lanes))
-                    masked = jnp.where(live, similar[:, place], neg_large)
-                    scores[turn, :, place] = masked
-                    running = jnp.maximum(running, masked)
-            highest = jnp.max(running, axis=1, keepdims=True)
-            total = jnp.zeros((block_rows, lanes), jnp.float32)
-            mean = jnp.zeros((block_rows, width), jnp.float32)
-            for turn, (source, base) in enumerate(sources):
-                coarse, fine = [], []
-                for place in places:
-                    terms = jnp.exp2((scores[turn, :, place] - highest) * inv_tau_log2)
-                    total = total + terms
-                    coarse.append(terms.astype(jnp.bfloat16))
-                    fine.append((terms - coarse[-1].astype(jnp.float32)).astype(jnp.bfloat16))
-                for part in (coarse, fine):
-                    mean = mean + contract(jnp.concatenate(part, axis=1), source[page], 1, 0)
-            total = jnp.sum(total, axis=1, keepdims=True)
-            mean = mean * (1.0 / total)
+            mean, highest, total = page_softmax(token_rows, sources, page, count, scores)
             for i in range(block_peers):
                 line = (b * block_peers + i) * lines + index * share
                 out[pl.ds(line, share)] = mean[i * share : (i + 1) * share]
-            any_live = count > (slot - parity) * patch_local
             log_count = jnp.log(count.astype(jnp.float32))
             for half in range(block_rows // lanes):
                 rows = slice(half * lanes, (half + 1) * lanes)
                 log_mean = jnp.log(as_row(total[rows])) - log_count
                 smooth = as_row(highest[rows]) + smooth_tau * log_mean
-                smooth = jnp.where(any_live, smooth, neg_large)
+                smooth = jnp.where(count > first_slot, smooth, neg_large)
                 line = pair_pages * share + (b * pair_pages + index) * (block_rows // lanes) + half
                 out[pl.ds(line, peers, stride=lines)] = jnp.broadcast_to(smooth, (peers, lanes))
 
@@ -163,7 +234,7 @@
         == lax.broadcasted_iota(jnp.int32, (lanes, lanes), 1) // query_len
     ).astype(jnp.bfloat16)
     group_ids = lax.broadcasted_iota(jnp.int32, (groups, lanes), 0)
-    position = lax.broadcasted_iota(jnp.int32, (chunk, block_rows), 0)
+    position = lax.broadcasted_iota(jnp.int32, (patch_local, block_rows), 0)
     pages = range(page_local)
 
     def sender(page, side):
@@ -229,14 +300,13 @@
             live_count = count - slot * patch_local
             page_weight = jnp.concatenate(row_weights[page], axis=1)
             page_lse = jnp.concatenate(row_lse[page], axis=1) + smooth_tau * log_row(count)
-            for start in range(0, patch_local, chunk):
-                similar = contract(own[page, start : start + chunk], token_rows, 1, 1)
-                coef = page_weight * jnp.exp2((similar - page_lse) * inv_tau_log2)
-                coef = jnp.where(position < live_count - start, coef, 0.0).astype(jnp.bfloat16)
-                grad = contract(coef, token_rows, 1, 0)
-                if tokens.shape[0] > block_queries:
-                    grad = grad + jnp.where(b == 0, 0.0, page_grad[page, start : start + chunk])
-                page_grad[page, start : start + chunk] = grad
+            similar = contract(own[page], token_rows, 1, 1)
+            coef = page_weight * jnp.exp2((similar - page_lse) * inv_tau_log2)
+            coef = jnp.where(position < live_count, coef, 0.0).astype(jnp.bfloat16)
+            grad = contract(coef, token_rows, 1, 0)
+            if tokens.shape[0] > block_queries:
+                grad = grad + jnp.where(b == 0, 0.0, page_grad[page])
+            page_grad[page] = grad
 
         def own_rows():
             row = lax.rem(group, block_queries) * query_len + slot * share
@@ -271,12 +341,12 @@
     over_blocks(tokens.shape[0] // block_queries, block)
 
 
-def fetch_pairs(page_groups, slots, shifts):
+def fetch_pairs(page_groups, slots, index):
     return [
-        (group * slots + slot, (group ^ shifts[slot % 2]) * slots + slot)
+        (group * slots + slot, (group ^ shift) * slots + slot)
+        for slot in range(slots)
+        for shift in fetches[slot % 2][index : index + 1]
         for group in range(page_groups)
-        for slot in range(slots)
-        if shifts[slot % 2]
     ]
 
 
@@ -299,10 +369,10 @@
     scores = pltpu.VMEM((2, block_rows, patch_local), jnp.float32)
     small = pltpu.CompilerParams(vmem_limit_bytes=4 << 20)
     integer_shape = jax.ShapeDtypeStruct((page_local + 1, query_count * query_len), jnp.int32)
-    if page_groups == 1 + sum(1 for side in fetches for shift in side if shift):
+    if page_local == 2 and page_groups == 1 + sum(len(side) for side in fetches):
         fetched = [
-            lax.ppermute(query_tokens, both, fetch_pairs(page_groups, slots, shifts))
-            for shifts in zip(*fetches)
+            lax.ppermute(query_tokens, both, fetch_pairs(page_groups, slots, i))
+            for i in range(len(fetches[1]))
         ]
         held = pl.pallas_call(
             hold_kernel,
@@ -313,28 +383,43 @@
             cost_estimate=pl.CostEstimate(flops=0, bytes_accessed=1 << 24, transcendentals=0),
             name="hold",
         )(page_patches)
-        gathered, mine, integers = pl.pallas_call(
+        gathered = pl.pallas_call(
             gather_kernel,
+            out_shape=jax.ShapeDtypeStruct((len(fetched), query_len, width), query_tokens.dtype),
+            in_specs=[vmem] * (len(fetched) + 1),
+            out_specs=vmem,
+            compiler_params=small,
+            name="gather",
+        )(held, *fetched)
+        others = lax.ppermute(gathered, "queries", [(i, i ^ 1) for i in range(slots)])
+        near = len(fetched) - 1
+        half_scores = pltpu.VMEM((2, block_rows // 2, patch_local), jnp.float32)
+        means, rows, integers = pl.pallas_call(
+            early_kernel,
             out_shape=(
-                jax.ShapeDtypeStruct((len(fetched), query_len, width), query_tokens.dtype),
-                jax.ShapeDtypeStruct(query_tokens.shape, query_tokens.dtype),
+                jax.ShapeDtypeStruct((near + 1, query_len, width), jnp.float32),
+                jax.ShapeDtypeStruct((2, block_rows // lanes, lanes), jnp.float32),
                 integer_shape,
             ),
-            in_specs=[vmem] * (len(fetched) + 4),
+            in_specs=[vmem] * (5 + near),
             out_specs=(vmem, vmem, vmem),
-            compiler_params=small,
-            name="gather",
-        )(patch_counts, positive_page, held, query_tokens, *fetched)
-        others = lax.ppermute(gathered, "queries", [(i, i ^ 1) for i in range(slots)])
+            scratch_shapes=[half_scores],
+            compiler_params=params,
+            cost_estimate=pl.CostEstimate(flops=0, bytes_accessed=1 << 24, transcendentals=0),
+            name="early",
+        )(patch_counts, positive_page, held, partner, query_tokens, *fetched[:near])
         told, tokens = pl.pallas_call(
-            functools.partial(assembled_kernel, share, lines),
-            out_shape=(told_shape, token_shape),
-            in_specs=[vmem] * (5 + len(fetched)),
+            functools.partial(late_kernel, share),
+            out_shape=(
+                jax.ShapeDtypeStruct((page_groups, slots * lines, lanes), jnp.float32),
+                token_shape,
+            ),
+            in_specs=[vmem] * (7 + len(fetched)),
             out_specs=(vmem, vmem),
-            scratch_shapes=[scores],
+            scratch_shapes=[half_scores],
             compiler_params=params,
-            name="forward",
-        )(integers, held, partner, mine, *fetched, others)
+            name="late",
+        )(integers, held, partner, means, rows, query_tokens, *fetched, others)
     else:
         tokens = lax.all_to_all(
             jnp.broadcast_to(query_tokens, token_shape.shape), "pages", 0, 0, tiled=True

time: 27.7 us -> 27.2 us (0.982)
  waiting for transfers between devices: 3.56 us -> 2.95 us
    ppermute x1, waiting for transfers between devices: 0.86 us -> 0.28 us  [shards(): lax.ppermute(gathered, 'queries', [(i, i ^ 1) for i in range(slots)])]
    pallas_call x2 -> x3, Pallas kernels: 0.82 us -> 1.09 us  [the longest x1 0.55 us: shards(): pl.pallas_call(early_kernel, out_shape=(jax.ShapeDtypeStruct((near + 1, q...]
  transfers between devices with their start and end apart: 6 -> 6, of which waited for: 3 -> 3; matrix products, arithmetic and copies ran while one was open for 0% -> 0% of each run, Pallas kernels for 0% -> 2%
where the time goes in v5:
time: 27.2 us; the launch traced here: 27 us
  blocking collectives  10.4 us (38%)
  starting transfers between devices  9.57 us (35%)
  waiting for transfers between devices  2.95 us (11%)
  Pallas kernels  2.42 us (9%)
  local copies, waits for them, and re-layouts  0.94 us (3%)
  between operations  0.71 us (3%)
    all_to_all x1, blocking collectives, shards(): lax.all_to_all(told, both, 0, 0, tiled=True).reshape(peers * lines, lanes)  10.4 us
    ppermute x4, starting transfers between devices, shards(): lax.ppermute(query_tokens, both, fetch_pairs(page_groups, slots, i))  8.05 us
    ppermute x4, waiting for transfers between devices, shards(): lax.ppermute(query_tokens, both, fetch_pairs(page_groups, slots, i))  2.67 us
    pallas_call x1, Pallas kernels, shards(): pl.pallas_call(functools.partial(backward_kernel, slots, share, lines), o...  1.31 us
    ppermute x1, starting transfers between devices, shards(): lax.ppermute(gathered, 'queries', [(i, i ^ 1) for i in range(slots)])  1 us
    unnamed x8, local copies, waits for them, and re-layouts  0.94 us
    pallas_call x1, Pallas kernels, shards(): pl.pallas_call(early_kernel, out_shape=(jax.ShapeDtypeStruct((near + 1, q...  0.55 us
  transfers between devices with their start and end apart: 6, of which 3 were waited for; matrix products, arithmetic and copies ran while one was open for 0% of the time, Pallas kernels for 2%

profile of v5, /device:TPU:0, one launch (start us, length us, event | category | flops | bytes accessed | tf_op | source)
XLA Modules:
  0.0 27.0 jit_solution(16546107589207851785)
XLA Ops:
  0.6 0.5 %collective-permute-start = (bf16[2,384,128]{2,1,0:T(8,128)(2,1)}, bf16[2,384,128]{2,1,0:T(8,128)(2,1)S(1)}, u32[]{:S(2)}, u32[]{:S(2)}) collective-permute-start(bf16[2,384,128]{2,1,0:T(8,128)(2,1)} %patches.1), channel_id=1, source_target_pairs={{0,1},{1,0},{2,3},{3,2},{4,5},{5,4},{6,7},{7,6},{8,9},{9,8},{10,11... | collective-permute-start | bytes 589832 | tf_op jit(solution)/shard_map/ppermute | solution.py:366
  1.1 2.6 %collective-permute-start.3 = (bf16[1,32,128]{2,1,0:T(8,128)(2,1)}, bf16[1,32,128]{2,1,0:T(8,128)(2,1)S(1)}, u32[]{:S(2)}, u32[]{:S(2)}) collective-permute-start(bf16[1,32,128]{2,1,0:T(8,128)(2,1)} %mine.3), channel_id=1, source_target_pairs={{0,8},{4,12},{8,0},{12,4},{16,24},{20,28},{24,16},{28,20},{1,13},{... | collective-permute-start | bytes 24584 | tf_op jit(solution)/shard_map/ppermute | solution.py:374
  3.8 3.4 %collective-permute-start.2 = (bf16[1,32,128]{2,1,0:T(8,128)(2,1)}, bf16[1,32,128]{2,1,0:T(8,128)(2,1)S(1)}, u32[]{:S(2)}, u32[]{:S(2)}) collective-permute-start(bf16[1,32,128]{2,1,0:T(8,128)(2,1)} %mine.3), channel_id=1, source_target_pairs={{0,28},{4,24},{8,20},{12,16},{16,12},{20,8},{24,4},{28,0},{1,5},{5... | collective-permute-start | bytes 24584 | tf_op jit(solution)/shard_map/ppermute | solution.py:374
  7.2 1.3 %collective-permute-start.1 = (bf16[1,32,128]{2,1,0:T(8,128)(2,1)}, bf16[1,32,128]{2,1,0:T(8,128)(2,1)S(1)}, u32[]{:S(2)}, u32[]{:S(2)}) collective-permute-start(bf16[1,32,128]{2,1,0:T(8,128)(2,1)} %mine.3), channel_id=1, source_target_pairs={{0,24},{4,28},{8,16},{12,20},{16,8},{20,12},{24,0},{28,4},{1,21},{... | collective-permute-start | bytes 24584 | tf_op jit(solution)/shard_map/ppermute | solution.py:374
  8.5 0.6 %collective-permute-start.4 = (bf16[1,32,128]{2,1,0:T(8,128)(2,1)}, bf16[1,32,128]{2,1,0:T(8,128)(2,1)S(1)}, u32[]{:S(2)}, u32[]{:S(2)}) collective-permute-start(bf16[1,32,128]{2,1,0:T(8,128)(2,1)} %mine.3), channel_id=1, source_target_pairs={{1,17},{5,21},{9,25},{13,29},{17,1},{21,5},{25,9},{29,13},{3,19},{... | collective-permute-start | bytes 24584 | tf_op jit(solution)/shard_map/ppermute | solution.py:374
  9.2 0.0 copy-start
  9.2 0.9 %copy-done = bf16[2,384,128]{2,1,0:T(8,128)(2,1)S(1)} copy-done((bf16[2,384,128]{2,1,0:T(8,128)(2,1)S(1)}, bf16[2,384,128]{2,1,0:T(8,128)(2,1)}, u32[]{:S(2)}) %copy-start) | copy-done | bytes 196632
  10.2 0.0 copy-start.1
  10.2 0.0 copy-start.2
  10.2 0.0 copy-start.3
  10.2 0.0 collective-permute-done.3.refs_2_
  10.2 0.2 collective-permute-done.2.refs_1_
  10.4 2.5 %collective-permute-done.1.refs_0_ = bf16[1,32,128]{2,1,0:T(8,128)(2,1)S(1)} collective-permute-done((bf16[1,32,128]{2,1,0:T(8,128)(2,1)}, bf16[1,32,128]{2,1,0:T(8,128)(2,1)S(1)}, u32[]{:S(2)}, u32[]{:S(2)}) %collective-permute-start.1) | collective-permute-done | bytes 8224 | tf_op jit(solution)/shard_map/ppermute | solution.py:374
  12.9 0.0 collective-permute-done.4.refs_3_
  12.9 1.0 %collective-permute-start.5 = (bf16[4,32,128]{2,1,0:T(8,128)(2,1)S(1)}, bf16[4,32,128]{2,1,0:T(8,128)(2,1)S(1)}, u32[]{:S(2)}, u32[]{:S(2)}) collective-permute-start(bf16[4,32,128]{2,1,0:T(8,128)(2,1)S(1)} %gather.1), channel_id=1, source_target_pairs={{0,1},{1,0},{2,3},{3,2},{4,5},{5,4},{6,7},{7,6},{8,9},{9,8},{10,11... | collective-permute-start | bytes 98312 | tf_op jit(solution)/shard_map/ppermute | solution.py:394
  13.9 0.0 collective-permute-done.partner
  13.9 0.0 copy-done.1
  13.9 0.0 copy-done.2
  13.9 0.0 copy-done.3
  13.9 0.6 %early.1 = (f32[4,32,128]{2,1,0:T(8,128)S(1)}, f32[2,2,128]{2,1,0:T(2,128)S(1)}, s32[3,256]{1,0:T(4,128)S(1)}) custom-call(s32[2]{0:T(128)S(1)} %copy-done.2, s32[8]{0:T(128)S(1)} %copy-done.3, bf16[2,384,128]{2,1,0:T(8,128)(2,1)S(1)} %hold.1.own._, bf16[2,384,128]{2,1,0:T(8,128)(2,1)S(1)} %collective-permute-done.partner, ...), custom_call_target="tpu_custom_call" | custom-call | bytes 16777216 | tf_op jit(solution)/shard_map/early/pallas_call | solution.py:397
  14.4 0.3 %collective-permute-done.5.refs_4_ = bf16[4,32,128]{2,1,0:T(8,128)(2,1)S(1)} collective-permute-done((bf16[4,32,128]{2,1,0:T(8,128)(2,1)S(1)}, bf16[4,32,128]{2,1,0:T(8,128)(2,1)S(1)}, u32[]{:S(2)}, u32[]{:S(2)}) %collective-permute-start.5) | collective-permute-done | bytes 32800 | tf_op jit(solution)/shard_map/ppermute | solution.py:394
  14.7 0.5 %late.1 = (f32[8,40,128]{2,1,0:T(8,128)S(1)}, bf16[8,32,128]{2,1,0:T(8,128)(2,1)S(1)}) custom-call(s32[3,256]{1,0:T(4,128)S(1)} %get-tuple-element.8.integers, bf16[2,384,128]{2,1,0:T(8,128)(2,1)S(1)} %hold.1.own._, bf16[2,384,128]{2,1,0:T(8,128)(2,1)S(1)} %collective-permute-done.partner, f32[4,32,128]{2,1,0:T(8,128)S(1)} %get-tuple-element.9.early_means, ...), custom_call_target="tpu_custom_call" | custom-call | tf_op jit(solution)/shard_map/late/pallas_call | solution.py:411
  15.3 10.4 %all_to_all.5 = f32[32,5,2,128]{3,2,1,0:T(2,128)S(1)} all-to-all(f32[32,5,2,128]{3,2,1,0:T(2,128)S(1)} %bitcast.3), channel_id=1, replica_groups=mesh['pages'=8,'queries'=4] {'pages','queries'}, dimensions={0} | all-to-all | bytes 327680 | tf_op jit(solution)/shard_map/all_to_all | solution.py:446
  25.7 1.3 %backward.1 = (f32[8]{0:T(128)}, f32[1,8,128]{2,1,0:T(8,128)}, f32[2,384,128]{2,1,0:T(8,128)}) custom-call(s32[3,256]{1,0:T(4,128)S(1)} %get-tuple-element.8.integers, f32[320,128]{1,0:T(8,128)S(1)} %bitcast.2, bf16[8,32,128]{2,1,0:T(8,128)(2,1)S(1)} %get-tuple-element.12.tokens, bf16[2,384,128]{2,1,0:T(8,128)(2,1)S(1)} %hold.1.own._), custom_call_target="tpu_custom_call" | custom-call | tf_op jit(solution)/shard_map/backward/pallas_call | solution.py:447
  (2 shorter events, 0.0 us)
Async XLA Ops:
  0.6 13.2 %collective-permute-start = (bf16[2,384,128]{2,1,0:T(8,128)(2,1)}, bf16[2,384,128]{2,1,0:T(8,128)(2,1)S(1)}, u32[]{:S(2)}, u32[]{:S(2)}) collective-permute-start(bf16[2,384,128]{2,1,0:T(8,128)(2,1)} %patches.1), channel_id=1, source_target_pairs={{0,1},{1,0},{2,3},{3,2},{4,5},{5,4},{6,7},{7,6},{8,9},{9,8},{10,11... | collective-permute-start | bytes 589832 | tf_op jit(solution)/shard_map/ppermute | solution.py:366
  1.1 9.0 %collective-permute-start.3 = (bf16[1,32,128]{2,1,0:T(8,128)(2,1)}, bf16[1,32,128]{2,1,0:T(8,128)(2,1)S(1)}, u32[]{:S(2)}, u32[]{:S(2)}) collective-permute-start(bf16[1,32,128]{2,1,0:T(8,128)(2,1)} %mine.3), channel_id=1, source_target_pairs={{0,8},{4,12},{8,0},{12,4},{16,24},{20,28},{24,16},{28,20},{1,13},{... | collective-permute-start | bytes 24584 | tf_op jit(solution)/shard_map/ppermute | solution.py:374
  3.8 6.6 %collective-permute-start.2 = (bf16[1,32,128]{2,1,0:T(8,128)(2,1)}, bf16[1,32,128]{2,1,0:T(8,128)(2,1)S(1)}, u32[]{:S(2)}, u32[]{:S(2)}) collective-permute-start(bf16[1,32,128]{2,1,0:T(8,128)(2,1)} %mine.3), channel_id=1, source_target_pairs={{0,28},{4,24},{8,20},{12,16},{16,12},{20,8},{24,4},{28,0},{1,5},{5... | collective-permute-start | bytes 24584 | tf_op jit(solution)/shard_map/ppermute | solution.py:374
  7.2 5.7 %collective-permute-start.1 = (bf16[1,32,128]{2,1,0:T(8,128)(2,1)}, bf16[1,32,128]{2,1,0:T(8,128)(2,1)S(1)}, u32[]{:S(2)}, u32[]{:S(2)}) collective-permute-start(bf16[1,32,128]{2,1,0:T(8,128)(2,1)} %mine.3), channel_id=1, source_target_pairs={{0,24},{4,28},{8,16},{12,20},{16,8},{20,12},{24,0},{28,4},{1,21},{... | collective-permute-start | bytes 24584 | tf_op jit(solution)/shard_map/ppermute | solution.py:374
  8.5 4.3 %collective-permute-start.4 = (bf16[1,32,128]{2,1,0:T(8,128)(2,1)}, bf16[1,32,128]{2,1,0:T(8,128)(2,1)S(1)}, u32[]{:S(2)}, u32[]{:S(2)}) collective-permute-start(bf16[1,32,128]{2,1,0:T(8,128)(2,1)} %mine.3), channel_id=1, source_target_pairs={{1,17},{5,21},{9,25},{13,29},{17,1},{21,5},{25,9},{29,13},{3,19},{... | collective-permute-start | bytes 24584 | tf_op jit(solution)/shard_map/ppermute | solution.py:374
  9.2 0.9 %copy-start = (bf16[2,384,128]{2,1,0:T(8,128)(2,1)S(1)}, bf16[2,384,128]{2,1,0:T(8,128)(2,1)}, u32[]{:S(2)}) copy-start(bf16[2,384,128]{2,1,0:T(8,128)(2,1)} %patches.1) | copy-start | bytes 589828
  10.2 3.7 %copy-start.1 = (bf16[1,32,128]{2,1,0:T(8,128)(2,1)S(1)}, bf16[1,32,128]{2,1,0:T(8,128)(2,1)}, u32[]{:S(2)}) copy-start(bf16[1,32,128]{2,1,0:T(8,128)(2,1)} %mine.3) | copy-start | bytes 24580
  10.2 3.7 %copy-start.2 = (s32[2]{0:T(128)S(1)}, s32[2]{0:T(128)}, u32[]{:S(2)}) copy-start(s32[2]{0:T(128)} %counts.1) | copy-start | bytes 28
  10.2 3.7 %copy-start.3 = (s32[8]{0:T(128)S(1)}, s32[8]{0:T(128)}, u32[]{:S(2)}) copy-start(s32[8]{0:T(128)} %positive.1) | copy-start | bytes 100
  12.9 1.9 %collective-permute-start.5 = (bf16[4,32,128]{2,1,0:T(8,128)(2,1)S(1)}, bf16[4,32,128]{2,1,0:T(8,128)(2,1)S(1)}, u32[]{:S(2)}, u32[]{:S(2)}) collective-permute-start(bf16[4,32,128]{2,1,0:T(8,128)(2,1)S(1)} %gather.1), channel_id=1, source_target_pairs={{0,1},{1,0},{2,3},{3,2},{4,5},{5,4},{6,7},{7,6},{8,9},{9,8},{10,11... | collective-permute-start | bytes 98312 | tf_op jit(solution)/shard_map/ppermute | solution.py:394

commit v6 on v5

--- a/solution.py
+++ b/solution.py
@@ -17,7 +17,7 @@
 lanes = 128
 block_rows = 256
 both = ("pages", "queries")
-fetches = ((6, 7, 2), (5, 1, 3, 4))
+fetches = ((6, 2, 7), (3, 5, 1, 4))
 
 
 def contract(a, b, dim_a, dim_b):
@@ -176,11 +176,11 @@
     highest, total = highest + early_lines[0], total + early_lines[1]
     smooth = highest + smooth_tau * (jnp.log(total) - jnp.log(count.astype(jnp.float32)))
     smooth = jnp.where(count > first_slot, smooth, neg_large)
-    peers = out.shape[0] * out.shape[1] // lines
-    flat = out.reshape(peers * lines, lanes)
     for half in range(smooth.shape[0]):
-        row = jnp.broadcast_to(smooth[half : half + 1], (peers, lanes))
-        flat[pl.ds(share + half, peers, stride=lines)] = row
+        row = jnp.broadcast_to(smooth[half : half + 1][None], (out.shape[0], 1, lanes))
+        for k in range(query_len // share):
+            line = k * lines + share + half
+            out[:, line : line + 1] = row
 
 
 def forward_kernel(share, lines, integers, tokens, own, partner, out, scores):
@@ -345,7 +345,7 @@
     return [
         (group * slots + slot, (group ^ shift) * slots + slot)
         for slot in range(slots)
-        for shift in fetches[slot % 2][index : index + 1]
+        for shift in (fetches[slot % 2] + (0,))[index : index + 1]
         for group in range(page_groups)
     ]
 
@@ -380,7 +380,6 @@
             in_specs=[vmem],
             out_specs=vmem,
             compiler_params=small,
-            cost_estimate=pl.CostEstimate(flops=0, bytes_accessed=1 << 24, transcendentals=0),
             name="hold",
         )(page_patches)
         gathered = pl.pallas_call(
@@ -405,7 +404,6 @@
             out_specs=(vmem, vmem, vmem),
             scratch_shapes=[half_scores],
             compiler_params=params,
-            cost_estimate=pl.CostEstimate(flops=0, bytes_accessed=1 << 24, transcendentals=0),
             name="early",
         )(patch_counts, positive_page, held, partner, query_tokens, *fetched[:near])
         told, tokens = pl.pallas_call(

time: 27.2 us -> 27.1 us (level)
    ppermute x1, starting transfers between devices: 1 us -> 1.45 us  [shards(): lax.ppermute(gathered, 'queries', [(i, i ^ 1) for i in range(slots)])]
where the time goes in v6:
time: 27.1 us; the launch traced here: 26.9 us
  blocking collectives  10.3 us (38%)
  starting transfers between devices  9.81 us (36%)
  waiting for transfers between devices  2.71 us (10%)
  Pallas kernels  2.43 us (9%)
  local copies, waits for them, and re-layouts  0.95 us (4%)
  between operations  0.7 us (3%)
    all_to_all x1, blocking collectives, shards(): lax.all_to_all(told, both, 0, 0, tiled=True).reshape(peers * lines, lanes)  10.3 us
    ppermute x4, starting transfers between devices, shards(): lax.ppermute(query_tokens, both, fetch_pairs(page_groups, slots, i))  7.85 us
    ppermute x4, waiting for transfers between devices, shards(): lax.ppermute(query_tokens, both, fetch_pairs(page_groups, slots, i))  2.43 us
    ppermute x1, starting transfers between devices, shards(): lax.ppermute(gathered, 'queries', [(i, i ^ 1) for i in range(slots)])  1.45 us
    pallas_call x1, Pallas kernels, shards(): pl.pallas_call(functools.partial(backward_kernel, slots, share, lines), o...  1.31 us
    unnamed x8, local copies, waits for them, and re-layouts  0.95 us
    pallas_call x1, Pallas kernels, shards(): pl.pallas_call(early_kernel, out_shape=(jax.ShapeDtypeStruct((near + 1, q...  0.56 us
    pallas_call x1, Pallas kernels, shards(): pl.pallas_call(functools.partial(late_kernel, share), out_shape=(jax.Shap...  0.54 us
  transfers between devices with their start and end apart: 6, of which 3 were waited for; matrix products, arithmetic and copies ran while one was open for 0% of the time, Pallas kernels for 2%

profile of v6, /device:TPU:0, one launch (start us, length us, event | category | flops | bytes accessed | tf_op | source)
XLA Modules:
  0.0 26.9 jit_solution(12577515555277648028)
XLA Ops:
  0.6 0.5 %collective-permute-start = (bf16[2,384,128]{2,1,0:T(8,128)(2,1)}, bf16[2,384,128]{2,1,0:T(8,128)(2,1)S(1)}, u32[]{:S(2)}, u32[]{:S(2)}) collective-permute-start(bf16[2,384,128]{2,1,0:T(8,128)(2,1)} %patches.1), channel_id=1, source_target_pairs={{0,1},{1,0},{2,3},{3,2},{4,5},{5,4},{6,7},{7,6},{8,9},{9,8},{10,11... | collective-permute-start | bytes 589832 | tf_op jit(solution)/shard_map/ppermute | solution.py:366
  1.1 5.6 %collective-permute-start.3 = (bf16[1,32,128]{2,1,0:T(8,128)(2,1)}, bf16[1,32,128]{2,1,0:T(8,128)(2,1)S(1)}, u32[]{:S(2)}, u32[]{:S(2)}) collective-permute-start(bf16[1,32,128]{2,1,0:T(8,128)(2,1)} %mine.3), channel_id=1, source_target_pairs={{0,28},{4,24},{8,20},{12,16},{16,12},{20,8},{24,4},{28,0},{1,5},{5... | collective-permute-start | bytes 24584 | tf_op jit(solution)/shard_map/ppermute | solution.py:374
  6.8 0.0 collective-permute-start.2
  6.8 0.9 %collective-permute-start.1 = (bf16[1,32,128]{2,1,0:T(8,128)(2,1)}, bf16[1,32,128]{2,1,0:T(8,128)(2,1)S(1)}, u32[]{:S(2)}, u32[]{:S(2)}) collective-permute-start(bf16[1,32,128]{2,1,0:T(8,128)(2,1)} %mine.3), channel_id=1, source_target_pairs={{0,24},{4,28},{8,16},{12,20},{16,8},{20,12},{24,0},{28,4},{1,13},{... | collective-permute-start | bytes 24584 | tf_op jit(solution)/shard_map/ppermute | solution.py:374
  7.7 1.3 %collective-permute-start.4 = (bf16[1,32,128]{2,1,0:T(8,128)(2,1)}, bf16[1,32,128]{2,1,0:T(8,128)(2,1)S(1)}, u32[]{:S(2)}, u32[]{:S(2)}) collective-permute-start(bf16[1,32,128]{2,1,0:T(8,128)(2,1)} %mine.3), channel_id=1, source_target_pairs={{0,0},{4,4},{8,8},{12,12},{16,16},{20,20},{24,24},{28,28},{1,17},{... | collective-permute-start | bytes 24584 | tf_op jit(solution)/shard_map/ppermute | solution.py:374
  9.0 0.0 copy-start
  9.0 0.9 %copy-done = bf16[2,384,128]{2,1,0:T(8,128)(2,1)S(1)} copy-done((bf16[2,384,128]{2,1,0:T(8,128)(2,1)S(1)}, bf16[2,384,128]{2,1,0:T(8,128)(2,1)}, u32[]{:S(2)}) %copy-start) | copy-done | bytes 196632
  9.9 0.0 copy-start.1
  10.0 0.0 copy-start.2
  10.0 0.0 copy-start.3
  10.0 0.0 collective-permute-done.3.refs_2_
  10.0 0.6 %collective-permute-done.2.refs_1_ = bf16[1,32,128]{2,1,0:T(8,128)(2,1)S(1)} collective-permute-done((bf16[1,32,128]{2,1,0:T(8,128)(2,1)}, bf16[1,32,128]{2,1,0:T(8,128)(2,1)S(1)}, u32[]{:S(2)}, u32[]{:S(2)}) %collective-permute-start.2) | collective-permute-done | bytes 8224 | tf_op jit(solution)/shard_map/ppermute | solution.py:374
  10.6 1.8 %collective-permute-done.1.refs_0_ = bf16[1,32,128]{2,1,0:T(8,128)(2,1)S(1)} collective-permute-done((bf16[1,32,128]{2,1,0:T(8,128)(2,1)}, bf16[1,32,128]{2,1,0:T(8,128)(2,1)S(1)}, u32[]{:S(2)}, u32[]{:S(2)}) %collective-permute-start.1) | collective-permute-done | bytes 8224 | tf_op jit(solution)/shard_map/ppermute | solution.py:374
  12.4 0.0 collective-permute-done.4.refs_3_
  12.4 1.4 %collective-permute-start.5 = (bf16[4,32,128]{2,1,0:T(8,128)(2,1)S(1)}, bf16[4,32,128]{2,1,0:T(8,128)(2,1)S(1)}, u32[]{:S(2)}, u32[]{:S(2)}) collective-permute-start(bf16[4,32,128]{2,1,0:T(8,128)(2,1)S(1)} %gather.1), channel_id=1, source_target_pairs={{0,1},{1,0},{2,3},{3,2},{4,5},{5,4},{6,7},{7,6},{8,9},{9,8},{10,11... | collective-permute-start | bytes 98312 | tf_op jit(solution)/shard_map/ppermute | solution.py:393
  13.9 0.0 collective-permute-done.partner
  13.9 0.0 copy-done.1
  13.9 0.0 copy-done.2
  13.9 0.0 copy-done.3
  13.9 0.6 %early.1 = (f32[4,32,128]{2,1,0:T(8,128)S(1)}, f32[2,2,128]{2,1,0:T(2,128)S(1)}, s32[3,256]{1,0:T(4,128)S(1)}) custom-call(s32[2]{0:T(128)S(1)} %copy-done.2, s32[8]{0:T(128)S(1)} %copy-done.3, bf16[2,384,128]{2,1,0:T(8,128)(2,1)S(1)} %hold.1.own._, bf16[2,384,128]{2,1,0:T(8,128)(2,1)S(1)} %collective-permute-done.partner, ...), custom_call_target="tpu_custom_call" | custom-call | tf_op jit(solution)/shard_map/early/pallas_call | solution.py:396
  14.5 0.3 %collective-permute-done.5.refs_4_ = bf16[4,32,128]{2,1,0:T(8,128)(2,1)S(1)} collective-permute-done((bf16[4,32,128]{2,1,0:T(8,128)(2,1)S(1)}, bf16[4,32,128]{2,1,0:T(8,128)(2,1)S(1)}, u32[]{:S(2)}, u32[]{:S(2)}) %collective-permute-start.5) | collective-permute-done | bytes 32800 | tf_op jit(solution)/shard_map/ppermute | solution.py:393
  14.7 0.5 %late.1 = (f32[8,40,128]{2,1,0:T(8,128)S(1)}, bf16[8,32,128]{2,1,0:T(8,128)(2,1)S(1)}) custom-call(s32[3,256]{1,0:T(4,128)S(1)} %get-tuple-element.8.integers, bf16[2,384,128]{2,1,0:T(8,128)(2,1)S(1)} %hold.1.own._, bf16[2,384,128]{2,1,0:T(8,128)(2,1)S(1)} %collective-permute-done.partner, f32[4,32,128]{2,1,0:T(8,128)S(1)} %get-tuple-element.9.early_means, ...), custom_call_target="tpu_custom_call" | custom-call | tf_op jit(solution)/shard_map/late/pallas_call | solution.py:409
  15.3 10.3 %all_to_all.5 = f32[32,5,2,128]{3,2,1,0:T(2,128)S(1)} all-to-all(f32[32,5,2,128]{3,2,1,0:T(2,128)S(1)} %bitcast.3), channel_id=1, replica_groups=mesh['pages'=8,'queries'=4] {'pages','queries'}, dimensions={0} | all-to-all | bytes 327680 | tf_op jit(solution)/shard_map/all_to_all | solution.py:444
  25.6 1.3 %backward.1 = (f32[8]{0:T(128)}, f32[1,8,128]{2,1,0:T(8,128)}, f32[2,384,128]{2,1,0:T(8,128)}) custom-call(s32[3,256]{1,0:T(4,128)S(1)} %get-tuple-element.8.integers, f32[320,128]{1,0:T(8,128)S(1)} %bitcast.2, bf16[8,32,128]{2,1,0:T(8,128)(2,1)S(1)} %get-tuple-element.12.tokens, bf16[2,384,128]{2,1,0:T(8,128)(2,1)S(1)} %hold.1.own._), custom_call_target="tpu_custom_call" | custom-call | tf_op jit(solution)/shard_map/backward/pallas_call | solution.py:445
  (2 shorter events, 0.0 us)
Async XLA Ops:
  0.6 13.2 %collective-permute-start = (bf16[2,384,128]{2,1,0:T(8,128)(2,1)}, bf16[2,384,128]{2,1,0:T(8,128)(2,1)S(1)}, u32[]{:S(2)}, u32[]{:S(2)}) collective-permute-start(bf16[2,384,128]{2,1,0:T(8,128)(2,1)} %patches.1), channel_id=1, source_target_pairs={{0,1},{1,0},{2,3},{3,2},{4,5},{5,4},{6,7},{7,6},{8,9},{9,8},{10,11... | collective-permute-start | bytes 589832 | tf_op jit(solution)/shard_map/ppermute | solution.py:366
  1.1 8.8 %collective-permute-start.3 = (bf16[1,32,128]{2,1,0:T(8,128)(2,1)}, bf16[1,32,128]{2,1,0:T(8,128)(2,1)S(1)}, u32[]{:S(2)}, u32[]{:S(2)}) collective-permute-start(bf16[1,32,128]{2,1,0:T(8,128)(2,1)} %mine.3), channel_id=1, source_target_pairs={{0,28},{4,24},{8,20},{12,16},{16,12},{20,8},{24,4},{28,0},{1,5},{5... | collective-permute-start | bytes 24584 | tf_op jit(solution)/shard_map/ppermute | solution.py:374
  6.8 3.9 %collective-permute-start.2 = (bf16[1,32,128]{2,1,0:T(8,128)(2,1)}, bf16[1,32,128]{2,1,0:T(8,128)(2,1)S(1)}, u32[]{:S(2)}, u32[]{:S(2)}) collective-permute-start(bf16[1,32,128]{2,1,0:T(8,128)(2,1)} %mine.3), channel_id=1, source_target_pairs={{0,8},{4,12},{8,0},{12,4},{16,24},{20,28},{24,16},{28,20},{1,21},{... | collective-permute-start | bytes 24584 | tf_op jit(solution)/shard_map/ppermute | solution.py:374
  6.8 5.7 %collective-permute-start.1 = (bf16[1,32,128]{2,1,0:T(8,128)(2,1)}, bf16[1,32,128]{2,1,0:T(8,128)(2,1)S(1)}, u32[]{:S(2)}, u32[]{:S(2)}) collective-permute-start(bf16[1,32,128]{2,1,0:T(8,128)(2,1)} %mine.3), channel_id=1, source_target_pairs={{0,24},{4,28},{8,16},{12,20},{16,8},{20,12},{24,0},{28,4},{1,13},{... | collective-permute-start | bytes 24584 | tf_op jit(solution)/shard_map/ppermute | solution.py:374
  7.7 4.8 %collective-permute-start.4 = (bf16[1,32,128]{2,1,0:T(8,128)(2,1)}, bf16[1,32,128]{2,1,0:T(8,128)(2,1)S(1)}, u32[]{:S(2)}, u32[]{:S(2)}) collective-permute-start(bf16[1,32,128]{2,1,0:T(8,128)(2,1)} %mine.3), channel_id=1, source_target_pairs={{0,0},{4,4},{8,8},{12,12},{16,16},{20,20},{24,24},{28,28},{1,17},{... | collective-permute-start | bytes 24584 | tf_op jit(solution)/shard_map/ppermute | solution.py:374
  9.0 0.9 %copy-start = (bf16[2,384,128]{2,1,0:T(8,128)(2,1)S(1)}, bf16[2,384,128]{2,1,0:T(8,128)(2,1)}, u32[]{:S(2)}) copy-start(bf16[2,384,128]{2,1,0:T(8,128)(2,1)} %patches.1) | copy-start | bytes 589828
  9.9 3.9 %copy-start.1 = (bf16[1,32,128]{2,1,0:T(8,128)(2,1)S(1)}, bf16[1,32,128]{2,1,0:T(8,128)(2,1)}, u32[]{:S(2)}) copy-start(bf16[1,32,128]{2,1,0:T(8,128)(2,1)} %mine.3) | copy-start | bytes 24580
  10.0 3.9 %copy-start.2 = (s32[2]{0:T(128)S(1)}, s32[2]{0:T(128)}, u32[]{:S(2)}) copy-start(s32[2]{0:T(128)} %counts.1) | copy-start | bytes 28
  10.0 3.9 %copy-start.3 = (s32[8]{0:T(128)S(1)}, s32[8]{0:T(128)}, u32[]{:S(2)}) copy-start(s32[8]{0:T(128)} %positive.1) | copy-start | bytes 100
  12.4 2.3 %collective-permute-start.5 = (bf16[4,32,128]{2,1,0:T(8,128)(2,1)S(1)}, bf16[4,32,128]{2,1,0:T(8,128)(2,1)S(1)}, u32[]{:S(2)}, u32[]{:S(2)}) collective-permute-start(bf16[4,32,128]{2,1,0:T(8,128)(2,1)S(1)} %gather.1), channel_id=1, source_target_pairs={{0,1},{1,0},{2,3},{3,2},{4,5},{5,4},{6,7},{7,6},{8,9},{9,8},{10,11... | collective-permute-start | bytes 98312 | tf_op jit(solution)/shard_map/ppermute | solution.py:393

commit v7 on v6

--- a/solution.py
+++ b/solution.py
@@ -256,6 +256,7 @@
         row_weights = [[] for _ in pages]
         row_lse = [[] for _ in pages]
         shares = []
+        smooths, all_parts = [], []
         for half in range(halves):
             smooth = []
             parts = []
@@ -269,8 +270,14 @@
                 terms = [jnp.exp2((x - highest) * inv_tau_log2) for x in heights]
                 total = functools.reduce(jnp.add, terms)
                 smooth.append(highest + smooth_tau * jnp.log(total))
-                parts.append([x / total for x in terms])
-            sums = token_sums(jnp.concatenate(smooth, axis=0)) * inv_temp
+                inverse = 1.0 / total
+                parts.append([x * inverse for x in terms])
+            smooths.append(smooth)
+            all_parts.append(parts)
+        every = token_sums(jnp.concatenate([x for smooth in smooths for x in smooth], axis=0))
+        for half, (smooth, parts) in enumerate(zip(smooths, all_parts)):
+            first = half * page_local * groups
+            sums = every[first : first + page_local * groups] * inv_temp
             logits = [sums[page * groups : (page + 1) * groups] for page in pages]
             top = functools.reduce(jnp.maximum, logits)
             top = jnp.max(top, axis=0, keepdims=True)
@@ -286,8 +293,9 @@
             losses = top + jnp.log(total) - jnp.sum(found, axis=0, keepdims=True)
             for i in range(half_queries):
                 loss[first_query + i] = jnp.max(losses[:, i * query_len : (i + 1) * query_len])
+            inverse = 1.0 / total
             weights = [
-                (x / total - jnp.where(hit, 1.0, 0.0)) * inv_temp for hit, x in zip(hits, grown)
+                (x * inverse - jnp.where(hit, 1.0, 0.0)) * inv_temp for hit, x in zip(hits, grown)
             ]
             for page in pages:
                 row_weights[page].append(mine(weights[page]))
@@ -345,7 +353,7 @@
     return [
         (group * slots + slot, (group ^ shift) * slots + slot)
         for slot in range(slots)
-        for shift in (fetches[slot % 2] + (0,))[index : index + 1]
+        for shift in fetches[slot % 2][index : index + 1]
         for group in range(page_groups)
     ]
 

time: 27.1 us -> 27.1 us (level)
  starting transfers between devices: 9.81 us -> 9.12 us
  waiting for transfers between devices: 2.71 us -> 3.4 us
    ppermute x4, starting transfers between devices: 7.85 us -> 7.15 us  [shards(): lax.ppermute(query_tokens, both, fetch_pairs(page_groups, slots, i))]
    ppermute x4, waiting for transfers between devices: 2.43 us -> 3.12 us  [shards(): lax.ppermute(query_tokens, both, fetch_pairs(page_groups, slots, i))]
where the time goes in v7:
time: 27.1 us; the launch traced here: 26.9 us
  blocking collectives  10.3 us (38%)
  starting transfers between devices  9.12 us (34%)
  waiting for transfers between devices  3.4 us (13%)
  Pallas kernels  2.42 us (9%)
  local copies, waits for them, and re-layouts  0.94 us (3%)
  between operations  0.71 us (3%)
    all_to_all x1, blocking collectives, shards(): lax.all_to_all(told, both, 0, 0, tiled=True).reshape(peers * lines, lanes)  10.3 us
    ppermute x4, starting transfers between devices, shards(): lax.ppermute(query_tokens, both, fetch_pairs(page_groups, slots, i))  7.15 us
    ppermute x4, waiting for transfers between devices, shards(): lax.ppermute(query_tokens, both, fetch_pairs(page_groups, slots, i))  3.12 us
    ppermute x1, starting transfers between devices, shards(): lax.ppermute(gathered, 'queries', [(i, i ^ 1) for i in range(slots)])  1.45 us
    pallas_call x1, Pallas kernels, shards(): pl.pallas_call(functools.partial(backward_kernel, slots, share, lines), o...  1.3 us
    unnamed x8, local copies, waits for them, and re-layouts  0.94 us
    pallas_call x1, Pallas kernels, shards(): pl.pallas_call(early_kernel, out_shape=(jax.ShapeDtypeStruct((near + 1, q...  0.56 us
    pallas_call x1, Pallas kernels, shards(): pl.pallas_call(functools.partial(late_kernel, share), out_shape=(jax.Shap...  0.54 us
  transfers between devices with their start and end apart: 6, of which 3 were waited for; matrix products, arithmetic and copies ran while one was open for 0% of the time, Pallas kernels for 2%

profile of v7, /device:TPU:0, one launch (start us, length us, event | category | flops | bytes accessed | tf_op | source)
XLA Modules:
  0.0 26.9 jit_solution(18242472550314649079)
XLA Ops:
  0.6 0.5 %collective-permute-start = (bf16[2,384,128]{2,1,0:T(8,128)(2,1)}, bf16[2,384,128]{2,1,0:T(8,128)(2,1)S(1)}, u32[]{:S(2)}, u32[]{:S(2)}) collective-permute-start(bf16[2,384,128]{2,1,0:T(8,128)(2,1)} %patches.1), channel_id=1, source_target_pairs={{0,1},{1,0},{2,3},{3,2},{4,5},{5,4},{6,7},{7,6},{8,9},{9,8},{10,11... | collective-permute-start | bytes 589832 | tf_op jit(solution)/shard_map/ppermute | solution.py:374
  1.1 5.6 %collective-permute-start.3 = (bf16[1,32,128]{2,1,0:T(8,128)(2,1)}, bf16[1,32,128]{2,1,0:T(8,128)(2,1)S(1)}, u32[]{:S(2)}, u32[]{:S(2)}) collective-permute-start(bf16[1,32,128]{2,1,0:T(8,128)(2,1)} %mine.3), channel_id=1, source_target_pairs={{0,28},{4,24},{8,20},{12,16},{16,12},{20,8},{24,4},{28,0},{1,5},{5... | collective-permute-start | bytes 24584 | tf_op jit(solution)/shard_map/ppermute | solution.py:382
  6.8 0.0 collective-permute-start.2
  6.8 0.9 %collective-permute-start.1 = (bf16[1,32,128]{2,1,0:T(8,128)(2,1)}, bf16[1,32,128]{2,1,0:T(8,128)(2,1)S(1)}, u32[]{:S(2)}, u32[]{:S(2)}) collective-permute-start(bf16[1,32,128]{2,1,0:T(8,128)(2,1)} %mine.3), channel_id=1, source_target_pairs={{0,24},{4,28},{8,16},{12,20},{16,8},{20,12},{24,0},{28,4},{1,13},{... | collective-permute-start | bytes 24584 | tf_op jit(solution)/shard_map/ppermute | solution.py:382
  7.7 0.6 %collective-permute-start.4 = (bf16[1,32,128]{2,1,0:T(8,128)(2,1)}, bf16[1,32,128]{2,1,0:T(8,128)(2,1)S(1)}, u32[]{:S(2)}, u32[]{:S(2)}) collective-permute-start(bf16[1,32,128]{2,1,0:T(8,128)(2,1)} %mine.3), channel_id=1, source_target_pairs={{1,17},{5,21},{9,25},{13,29},{17,1},{21,5},{25,9},{29,13},{3,19},{... | collective-permute-start | bytes 24584 | tf_op jit(solution)/shard_map/ppermute | solution.py:382
  8.3 0.0 copy-start
  8.3 0.9 %copy-done = bf16[2,384,128]{2,1,0:T(8,128)(2,1)S(1)} copy-done((bf16[2,384,128]{2,1,0:T(8,128)(2,1)S(1)}, bf16[2,384,128]{2,1,0:T(8,128)(2,1)}, u32[]{:S(2)}) %copy-start) | copy-done | bytes 196632
  9.3 0.0 copy-start.1
  9.3 0.0 copy-start.2
  9.3 0.0 copy-start.3
  9.3 0.0 collective-permute-done.3.refs_2_
  9.3 1.3 %collective-permute-done.2.refs_1_ = bf16[1,32,128]{2,1,0:T(8,128)(2,1)S(1)} collective-permute-done((bf16[1,32,128]{2,1,0:T(8,128)(2,1)}, bf16[1,32,128]{2,1,0:T(8,128)(2,1)S(1)}, u32[]{:S(2)}, u32[]{:S(2)}) %collective-permute-start.2) | collective-permute-done | bytes 8224 | tf_op jit(solution)/shard_map/ppermute | solution.py:382
  10.6 1.8 %collective-permute-done.1.refs_0_ = bf16[1,32,128]{2,1,0:T(8,128)(2,1)S(1)} collective-permute-done((bf16[1,32,128]{2,1,0:T(8,128)(2,1)}, bf16[1,32,128]{2,1,0:T(8,128)(2,1)S(1)}, u32[]{:S(2)}, u32[]{:S(2)}) %collective-permute-start.1) | collective-permute-done | bytes 8224 | tf_op jit(solution)/shard_map/ppermute | solution.py:382
  12.4 0.0 collective-permute-done.4.refs_3_
  12.4 1.4 %collective-permute-start.5 = (bf16[4,32,128]{2,1,0:T(8,128)(2,1)S(1)}, bf16[4,32,128]{2,1,0:T(8,128)(2,1)S(1)}, u32[]{:S(2)}, u32[]{:S(2)}) collective-permute-start(bf16[4,32,128]{2,1,0:T(8,128)(2,1)S(1)} %gather.1), channel_id=1, source_target_pairs={{0,1},{1,0},{2,3},{3,2},{4,5},{5,4},{6,7},{7,6},{8,9},{9,8},{10,11... | collective-permute-start | bytes 98312 | tf_op jit(solution)/shard_map/ppermute | solution.py:401
  13.9 0.0 collective-permute-done.partner
  13.9 0.0 copy-done.1
  13.9 0.0 copy-done.2
  13.9 0.0 copy-done.3
  13.9 0.6 %early.1 = (f32[4,32,128]{2,1,0:T(8,128)S(1)}, f32[2,2,128]{2,1,0:T(2,128)S(1)}, s32[3,256]{1,0:T(4,128)S(1)}) custom-call(s32[2]{0:T(128)S(1)} %copy-done.2, s32[8]{0:T(128)S(1)} %copy-done.3, bf16[2,384,128]{2,1,0:T(8,128)(2,1)S(1)} %hold.1.own._, bf16[2,384,128]{2,1,0:T(8,128)(2,1)S(1)} %collective-permute-done.partner, ...), custom_call_target="tpu_custom_call" | custom-call | tf_op jit(solution)/shard_map/early/pallas_call | solution.py:404
  14.5 0.3 %collective-permute-done.5.refs_4_ = bf16[4,32,128]{2,1,0:T(8,128)(2,1)S(1)} collective-permute-done((bf16[4,32,128]{2,1,0:T(8,128)(2,1)S(1)}, bf16[4,32,128]{2,1,0:T(8,128)(2,1)S(1)}, u32[]{:S(2)}, u32[]{:S(2)}) %collective-permute-start.5) | collective-permute-done | bytes 32800 | tf_op jit(solution)/shard_map/ppermute | solution.py:401
  14.7 0.5 %late.1 = (f32[8,40,128]{2,1,0:T(8,128)S(1)}, bf16[8,32,128]{2,1,0:T(8,128)(2,1)S(1)}) custom-call(s32[3,256]{1,0:T(4,128)S(1)} %get-tuple-element.8.integers, bf16[2,384,128]{2,1,0:T(8,128)(2,1)S(1)} %hold.1.own._, bf16[2,384,128]{2,1,0:T(8,128)(2,1)S(1)} %collective-permute-done.partner, f32[4,32,128]{2,1,0:T(8,128)S(1)} %get-tuple-element.9.early_means, ...), custom_call_target="tpu_custom_call" | custom-call | tf_op jit(solution)/shard_map/late/pallas_call | solution.py:417
  15.3 10.3 %all_to_all.5 = f32[32,5,2,128]{3,2,1,0:T(2,128)S(1)} all-to-all(f32[32,5,2,128]{3,2,1,0:T(2,128)S(1)} %bitcast.3), channel_id=1, replica_groups=mesh['pages'=8,'queries'=4] {'pages','queries'}, dimensions={0} | all-to-all | bytes 327680 | tf_op jit(solution)/shard_map/all_to_all | solution.py:452
  25.6 1.3 %backward.1 = (f32[8]{0:T(128)}, f32[1,8,128]{2,1,0:T(8,128)}, f32[2,384,128]{2,1,0:T(8,128)}) custom-call(s32[3,256]{1,0:T(4,128)S(1)} %get-tuple-element.8.integers, f32[320,128]{1,0:T(8,128)S(1)} %bitcast.2, bf16[8,32,128]{2,1,0:T(8,128)(2,1)S(1)} %get-tuple-element.12.tokens, bf16[2,384,128]{2,1,0:T(8,128)(2,1)S(1)} %hold.1.own._), custom_call_target="tpu_custom_call" | custom-call | tf_op jit(solution)/shard_map/backward/pallas_call | solution.py:453
  (2 shorter events, 0.0 us)
Async XLA Ops:
  0.6 13.2 %collective-permute-start = (bf16[2,384,128]{2,1,0:T(8,128)(2,1)}, bf16[2,384,128]{2,1,0:T(8,128)(2,1)S(1)}, u32[]{:S(2)}, u32[]{:S(2)}) collective-permute-start(bf16[2,384,128]{2,1,0:T(8,128)(2,1)} %patches.1), channel_id=1, source_target_pairs={{0,1},{1,0},{2,3},{3,2},{4,5},{5,4},{6,7},{7,6},{8,9},{9,8},{10,11... | collective-permute-start | bytes 589832 | tf_op jit(solution)/shard_map/ppermute | solution.py:374
  1.1 8.1 %collective-permute-start.3 = (bf16[1,32,128]{2,1,0:T(8,128)(2,1)}, bf16[1,32,128]{2,1,0:T(8,128)(2,1)S(1)}, u32[]{:S(2)}, u32[]{:S(2)}) collective-permute-start(bf16[1,32,128]{2,1,0:T(8,128)(2,1)} %mine.3), channel_id=1, source_target_pairs={{0,28},{4,24},{8,20},{12,16},{16,12},{20,8},{24,4},{28,0},{1,5},{5... | collective-permute-start | bytes 24584 | tf_op jit(solution)/shard_map/ppermute | solution.py:382
  6.8 3.9 %collective-permute-start.2 = (bf16[1,32,128]{2,1,0:T(8,128)(2,1)}, bf16[1,32,128]{2,1,0:T(8,128)(2,1)S(1)}, u32[]{:S(2)}, u32[]{:S(2)}) collective-permute-start(bf16[1,32,128]{2,1,0:T(8,128)(2,1)} %mine.3), channel_id=1, source_target_pairs={{0,8},{4,12},{8,0},{12,4},{16,24},{20,28},{24,16},{28,20},{1,21},{... | collective-permute-start | bytes 24584 | tf_op jit(solution)/shard_map/ppermute | solution.py:382
  6.8 5.7 %collective-permute-start.1 = (bf16[1,32,128]{2,1,0:T(8,128)(2,1)}, bf16[1,32,128]{2,1,0:T(8,128)(2,1)S(1)}, u32[]{:S(2)}, u32[]{:S(2)}) collective-permute-start(bf16[1,32,128]{2,1,0:T(8,128)(2,1)} %mine.3), channel_id=1, source_target_pairs={{0,24},{4,28},{8,16},{12,20},{16,8},{20,12},{24,0},{28,4},{1,13},{... | collective-permute-start | bytes 24584 | tf_op jit(solution)/shard_map/ppermute | solution.py:382
  7.7 4.8 %collective-permute-start.4 = (bf16[1,32,128]{2,1,0:T(8,128)(2,1)}, bf16[1,32,128]{2,1,0:T(8,128)(2,1)S(1)}, u32[]{:S(2)}, u32[]{:S(2)}) collective-permute-start(bf16[1,32,128]{2,1,0:T(8,128)(2,1)} %mine.3), channel_id=1, source_target_pairs={{1,17},{5,21},{9,25},{13,29},{17,1},{21,5},{25,9},{29,13},{3,19},{... | collective-permute-start | bytes 24584 | tf_op jit(solution)/shard_map/ppermute | solution.py:382
  8.3 0.9 %copy-start = (bf16[2,384,128]{2,1,0:T(8,128)(2,1)S(1)}, bf16[2,384,128]{2,1,0:T(8,128)(2,1)}, u32[]{:S(2)}) copy-start(bf16[2,384,128]{2,1,0:T(8,128)(2,1)} %patches.1) | copy-start | bytes 589828
  9.3 4.6 %copy-start.1 = (bf16[1,32,128]{2,1,0:T(8,128)(2,1)S(1)}, bf16[1,32,128]{2,1,0:T(8,128)(2,1)}, u32[]{:S(2)}) copy-start(bf16[1,32,128]{2,1,0:T(8,128)(2,1)} %mine.3) | copy-start | bytes 24580
  9.3 4.6 %copy-start.2 = (s32[2]{0:T(128)S(1)}, s32[2]{0:T(128)}, u32[]{:S(2)}) copy-start(s32[2]{0:T(128)} %counts.1) | copy-start | bytes 28
  9.3 4.6 %copy-start.3 = (s32[8]{0:T(128)S(1)}, s32[8]{0:T(128)}, u32[]{:S(2)}) copy-start(s32[8]{0:T(128)} %positive.1) | copy-start | bytes 100
  12.4 2.3 %collective-permute-start.5 = (bf16[4,32,128]{2,1,0:T(8,128)(2,1)S(1)}, bf16[4,32,128]{2,1,0:T(8,128)(2,1)S(1)}, u32[]{:S(2)}, u32[]{:S(2)}) collective-permute-start(bf16[4,32,128]{2,1,0:T(8,128)(2,1)S(1)} %gather.1), channel_id=1, source_target_pairs={{0,1},{1,0},{2,3},{3,2},{4,5},{5,4},{6,7},{7,6},{8,9},{9,8},{10,11... | collective-permute-start | bytes 98312 | tf_op jit(solution)/shard_map/ppermute | solution.py:401
